TPU v7x, 512 devices: a whole 4x8x8 slice. The times are simulated.
512 devices in a mesh: occ: 16 (over x, z_lo, core), vir: 32 (over z_hi, y).
Axes of the slice: x: 4, y: 8, z: 8 (z_hi: 4, z_lo: 2; z = z_hi * 2 + z_lo), core: 2. Of those that a mesh axis runs over, the one named last changes fastest.
Arguments:
- amplitudes: float32 [64, 64, 1024], P('occ'), may hold values from -6 to 6
- integrals: float32 [256, 256, 1024], P('vir', 'occ'), may hold values from -0.53033006 to 0.53033006
- occ_energy: float32 [64], replicated, may hold values from -2 to -0.5
- vir_energy: float32 [256], replicated, may hold values from 0.5 to 3
- occ_irrep: int32 [64], replicated, may hold values from 0 to 7
- vir_irrep: int32 [256], replicated, may hold values from 0 to 7
- pair_irrep: int32 [1024], replicated, may hold values from 0 to 7
Outputs:
- update: float32 [64, 64, 256, 256], P('occ', None, 'vir')
All inputs are finite; a program needn't handle non-finite values.
Results may differ from a plain program's by a relative error of at most 0.00007.
Values sent between devices are 32-bit elements; how exact they have to be, the bound alone decides.
A program may use at most 128 MiB of HBM per device.

v0:
```python
import jax
import jax.numpy as jnp
from jax import lax
from jax.sharding import PartitionSpec as P


def local(amplitudes, integrals, occ_energy, vir_energy, occ_irrep, vir_irrep, pair_irrep):
    occ_rows = amplitudes.shape[0]
    vir_rows = integrals.shape[0]
    vir_cols = integrals.shape[1]
    occ_start = lax.axis_index("occ") * occ_rows
    vir_start = lax.axis_index("vir") * vir_rows
    col_start = lax.axis_index("occ") * vir_cols
    own_occ = lax.dynamic_slice_in_dim(occ_irrep, occ_start, occ_rows)
    pair_sym = jnp.bitwise_xor(own_occ[:, None], occ_irrep[None, :])
    masked_amp = jnp.where(
        pair_sym[:, :, None] == pair_irrep[None, None, :], amplitudes, jnp.float32(0.0)
    )
    own_vir = lax.dynamic_slice_in_dim(vir_irrep, vir_start, vir_rows)
    col_vir = lax.dynamic_slice_in_dim(vir_irrep, col_start, vir_cols)
    vir_sym = jnp.bitwise_xor(own_vir[:, None], col_vir[None, :])
    masked_int = jnp.where(
        vir_sym[:, :, None] == pair_irrep[None, None, :], integrals, jnp.float32(0.0)
    )
    ladder = jnp.einsum(
        "ijk,abk->ijab",
        masked_amp,
        lax.all_gather(masked_int, "occ", axis=1, tiled=True),
        precision=lax.Precision.HIGHEST,
        preferred_element_type=jnp.float32,
    )
    ladder_swap = lax.all_to_all(ladder, "occ", split_axis=1, concat_axis=0, tiled=True)
    occ_anti = ladder - jnp.transpose(ladder_swap, (1, 0, 2, 3))
    virt_swap = lax.all_to_all(occ_anti, "vir", split_axis=3, concat_axis=2, tiled=True)
    anti = occ_anti - jnp.transpose(virt_swap, (0, 1, 3, 2))
    own_occ_energy = lax.dynamic_slice_in_dim(occ_energy, occ_start, occ_rows)
    own_vir_energy = lax.dynamic_slice_in_dim(vir_energy, vir_start, vir_rows)
    denom = (
        own_occ_energy[:, None, None, None]
        + occ_energy[None, :, None, None]
        - own_vir_energy[None, None, :, None]
        - vir_energy[None, None, None, :]
    )
    return anti / denom


def solution(mesh):
    placed = (P("occ", None, None), P("vir", "occ", None), P(), P(), P(), P(), P())
    return jax.shard_map(
        local, mesh=mesh, in_specs=placed, out_specs=P("occ", None, "vir", None), check_vma=False
    )
```

profile of v0, /device:TPU:1, one launch (start us, length us, event | category | flops | bytes accessed | tf_op | source)
XLA Modules:
  0.0 246.2 jit_solution(7954433561039027111)
XLA Ops:
  6.5 0.0 copy-start.1
  6.5 0.0 all-gather.2.cloned.1.call-start
  6.5 0.8 dynamic_slice.17
  7.4 0.8 dynamic_slice.16
  8.1 0.1 broadcast_xor_fusion
  8.2 1.9 compare_select_fusion
  10.1 0.0 all-gather.2.cloned.1.call-update
  10.2 0.7 dynamic_slice.15
  10.9 0.7 broadcast_xor_fusion.1
  11.6 62.3 %all-gather.2.cloned.1.call-done = f32[8,256,1024]{2,1,0:T(8,128)} async-done(((f32[8,16,1024]{2,1,0:T(8,128)}), f32[8,256,1024]{2,1,0:T(8,128)}) %all-gather.2.cloned.1.call-update) | async-done | bytes 8388624 | tf_op jit(solution)/shard_map/all_gather | solution.py:28
  73.9 0.0 copy-done.1
  73.9 9.7 %fusion = f32[4,64,8,256]{3,1,2,0:T(8,128)S(1)} fusion(f32[8,256,1024]{2,1,0:T(8,128)} %all-gather.2.cloned.1.call-done, f32[4,64,1024]{2,1,0:T(8,128)S(1)} %copy-done.1, s32[1024]{0:T(1024)} %param.13, s32[4,64]{1,0:T(4,128)S(1)} %broadcast_xor_fusion.1), kind=kOutput, calls=%fused_computation | convolution fusion | flops 6442975232 | bytes 11539456 | tf_op jit(solution)/shard_map/ijk,abk->ijab/dot_general | solution.py:25
  83.6 0.0 copy-start
  83.6 1.2 copy.16
  84.8 31.6 %all_to_all.36 = f32[4,64,8,256]{3,2,0,1:T(8,128)S(1)} all-to-all(f32[4,64,8,256]{3,2,0,1:T(8,128)S(1)} %copy.16), channel_id=1, replica_groups=mesh['occ'=16,'vir'=32] {'occ'}, dimensions={1} | all-to-all | bytes 4194304 | tf_op jit(solution)/shard_map/all_to_all | solution.py:32
  116.4 0.0 copy-done
  116.4 0.8 copy.26
  117.2 1.8 all_to_all.29
  119.0 2.5 %bitcast_subtract_fusion.1 = f32[4,64,8,256]{3,1,2,0:T(8,128)S(1)} fusion(f32[4,64,8,256]{3,1,2,0:T(8,128)} %copy-done, f32[64,4,8,256]{3,0,2,1:T(8,128)} %all_to_all.29), kind=kLoop, calls=%fused_computation.4 | loop fusion | flops 524288 | bytes 6291456 | tf_op jit(solution)/shard_map/sub | solution.py:33
  121.5 4.5 %copy.18 = f32[4,64,8,256]{1,2,0,3:T(8,128)} copy(f32[4,64,8,256]{3,1,2,0:T(8,128)S(1)} %bitcast_subtract_fusion.1) | data formatting | bytes 4194304 | tf_op jit(solution)/shard_map/sub | solution.py:33
  126.0 5.5 %reshape.97 = f32[32,1,16384]{2,1,0:T(1,128)} reshape(f32[256,4,8,64]{3,2,1,0:T(8,128)} %bitcast.26) | data formatting | bytes 4194304
  131.4 0.0 copy-start.3
  131.4 0.0 copy-start.2
  131.5 11.9 %all-to-all-start.1 = ((f32[32,1,16384]{2,1,0:T(1,128)}), f32[32,1,16384]{2,1,0:T(1,128)}, u32[]{:S(2)}, u32[]{:S(2)}) async-start(f32[32,1,16384]{2,1,0:T(1,128)} %reshape.97), calls=%async_computation.1 | async-start | bytes 4194304 | tf_op jit(solution)/shard_map/all_to_all | solution.py:34
  143.4 0.0 copy-done.3
  143.4 0.1 dynamic_slice.18
  143.5 0.0 copy-done.2
  143.5 0.1 dynamic_slice.19
  143.6 0.1 broadcast_add_fusion
  143.6 0.1 broadcast_subtract_fusion
  143.7 67.2 %all-to-all-done.1 = f32[32,1,16384]{2,1,0:T(1,128)} async-done(((f32[32,1,16384]{2,1,0:T(1,128)}), f32[32,1,16384]{2,1,0:T(1,128)}, u32[]{:S(2)}, u32[]{:S(2)}) %all-to-all-start.1) | async-done | bytes 2097184 | tf_op jit(solution)/shard_map/all_to_all | solution.py:34
  210.9 0.6 broadcast.76
  211.5 8.7 %reduce = f32[32,16384]{1,0:T(8,128)} reduce(f32[32,1,16384]{2,1,0:T(1,128)} %all-to-all-done.1, f32[]{:T(128)} %broadcast.76), dimensions={1}, to_apply=%all_to_all.30.reduce_sub_computation | reduce | bytes 4194308 | tf_op jit(solution)/shard_map/all_to_all | solution.py:34
  220.2 4.2 %reshape.98 = f32[256,4,8,64]{3,2,1,0:T(8,128)} reshape(f32[32,16384]{1,0:T(8,128)} %reduce) | data formatting | bytes 4194304
  224.5 6.6 %copy.20 = f32[4,64,32,8,8]{1,4,3,2,0:T(8,128)} copy(f32[4,64,32,8,8]{1,3,0,4,2:T(8,128)} %bitcast.27) | data formatting | bytes 4194304 | tf_op jit(solution)/shard_map/all_to_all | solution.py:34
  231.1 3.8 %copy.21 = f32[4,64,256,8]{2,1,3,0:T(8,128)} copy(f32[4,64,256,8]{1,3,2,0:T(8,128)} %bitcast.28) | data formatting | bytes 4194304 | tf_op jit(solution)/shard_map/all_to_all | solution.py:34
  234.8 1.9 fusion.2
  236.8 2.5 %copy.22 = f32[4,64,8,256]{3,2,1,0:T(8,128)} copy(f32[4,64,8,256]{3,1,2,0:T(8,128)S(1)} %fusion.2) | data formatting | bytes 4194304 | tf_op jit(solution)/shard_map/div | solution.py:44
Async XLA Ops:
  6.5 67.4 %copy-start.1 = (f32[4,64,1024]{2,1,0:T(8,128)S(1)}, f32[4,64,1024]{2,1,0:T(8,128)}, u32[]{:S(2)}) copy-start(f32[4,64,1024]{2,1,0:T(8,128)} %param.7) | copy-start | bytes 3145732
  6.5 67.4 %all-gather.2.cloned.1.call-start = ((), (), s32[]{:S(2)}) async-start(), calls=%async_computation.2 | async-start | bytes 8912896 | tf_op jit(solution)/shard_map/all_gather | solution.py:28
  83.6 32.8 %copy-start = (f32[4,64,8,256]{3,1,2,0:T(8,128)}, f32[4,64,8,256]{3,1,2,0:T(8,128)S(1)}, u32[]{:S(2)}) copy-start(f32[4,64,8,256]{3,1,2,0:T(8,128)S(1)} %fusion) | copy-start | bytes 6291460
  131.4 11.9 %copy-start.3 = (f32[64]{0:T(128)S(1)}, f32[64]{0:T(128)}, u32[]{:S(2)}) copy-start(f32[64]{0:T(128)} %param.9) | copy-start | bytes 772
  131.4 12.0 %copy-start.2 = (f32[256]{0:T(256)S(1)}, f32[256]{0:T(256)}, u32[]{:S(2)}) copy-start(f32[256]{0:T(256)} %param.10) | copy-start | bytes 3076
  131.5 79.5 %all-to-all-start.1 = ((f32[32,1,16384]{2,1,0:T(1,128)}), f32[32,1,16384]{2,1,0:T(1,128)}, u32[]{:S(2)}, u32[]{:S(2)}) async-start(f32[32,1,16384]{2,1,0:T(1,128)} %reshape.97), calls=%async_computation.1 | async-start | bytes 4194304 | tf_op jit(solution)/shard_map/all_to_all | solution.py:34
Sparse Core Ops, SparseCore 0:
  10.3 63.5 all-gather.1
where the time goes:
time: 250 us; the launch traced here: 246 us
  waiting for transfers between devices  130 us (52%)
  local copies, waits for them, and re-layouts  33.9 us (14%)
  blocking collectives  31.6 us (13%)
  other arithmetic  16.1 us (6%)
  between operations  13.5 us (5%)
  starting transfers between devices  11.9 us (5%)
  matrix products  9.66 us (4%)
    all_to_all x1, waiting for transfers between devices, local(): lax.all_to_all(occ_anti, 'vir', split_axis=3, concat_axis=2, tiled=True)  67.2 us
    all_gather x1, waiting for transfers between devices, local(): lax.all_gather(masked_int, 'occ', axis=1, tiled=True)  62.3 us
    all_to_all x1, blocking collectives, local(): lax.all_to_all(ladder, 'occ', split_axis=1, concat_axis=0, tiled=True)  31.6 us
    all_to_all x1, starting transfers between devices, local(): lax.all_to_all(occ_anti, 'vir', split_axis=3, concat_axis=2, tiled=True)  11.9 us
    all_to_all x3, local copies, waits for them, and re-layouts, local(): lax.all_to_all(occ_anti, 'vir', split_axis=3, concat_axis=2, tiled=True)  10.9 us
    unnamed x10, local copies, waits for them, and re-layouts  9.7 us
    dot_general x1, matrix products, local(): jnp.einsum('ijk,abk->ijab', masked_amp, lax.all_gather(masked_int, 'occ',...  9.66 us
    all_to_all x1, other arithmetic, local(): lax.all_to_all(occ_anti, 'vir', split_axis=3, concat_axis=2, tiled=True)  8.75 us
  transfers between devices with their start and end apart: 2, of which 2 were waited for; matrix products, arithmetic and copies ran while one was open for 1% of the time, Pallas kernels for 0%

commit v1 on v0

--- a/solution.py
+++ b/solution.py
@@ -1,10 +1,380 @@
+import functools
+
 import jax
 import jax.numpy as jnp
 from jax import lax
+from jax.experimental import pallas as pl
+from jax.experimental.pallas import tpu as pltpu
 from jax.sharding import PartitionSpec as P
 
-
-def local(amplitudes, integrals, occ_energy, vir_energy, occ_irrep, vir_irrep, pair_irrep):
+MESH = pl.DeviceIdType.MESH
+F32 = jnp.float32
+BF16 = jnp.bfloat16
+
+LANES = 128
+TAIL = 64
+CAP = LANES + TAIL
+CHUNKS = 2
+
+OWN, XP, XM, X2 = (0, 0, 0), (1, 0, 0), (3, 0, 0), (2, 0, 0)
+Z, ZP, ZM, Z2 = (0, 1, 0), (1, 1, 0), (3, 1, 0), (2, 1, 0)
+CORE = (0, 0, 1)
+STAGES = (
+    ((OWN, None, Z), (OWN, None, XP), (OWN, None, XM), (OWN, None, CORE)),
+    ((Z, None, XP), (Z, None, XM), (XM, 0, XP), (XP, 1, XM), (Z, None, CORE), (XM, None, CORE), (XP, None, CORE)),
+    ((X2, 0, Z), (X2, 1, Z), (X2, 0, CORE), (X2, 1, CORE), (ZM, None, CORE), (ZP, None, CORE)),
+    ((Z2, 0, CORE), (Z2, 1, CORE)),
+)
+
+
+def gather_ops():
+    ops, arrived = [], {}
+    for tick in range(len(STAGES) + CHUNKS - 1):
+        for chunk in range(CHUNKS):
+            if not 0 <= tick - chunk < len(STAGES):
+                continue
+            for whose, half, route in STAGES[tick - chunk]:
+                there = tuple((k - r) % n for k, r, n in zip(whose, route, (4, 2, 2)))
+                after = []
+                if whose != OWN:
+                    for h in (0, 1, None):
+                        if (chunk, whose, h) in arrived and (half is None or h is None or h == half):
+                            after.append(arrived[chunk, whose, h])
+                arrived[chunk, there, half] = len(ops)
+                ops.append((chunk, whose, half, route, tuple(after)))
+    return ops
+
+
+GATHER = gather_ops()
+
+
+def split(x):
+    high = x.astype(BF16)
+    return high, (x - high.astype(F32)).astype(BF16)
+
+
+def dot_t(a, b):
+    return lax.dot_general(a, b, (((1,), (1,)), ((), ())), preferred_element_type=F32)
+
+
+def at_lane(row, index):
+    lane = lax.broadcasted_iota(jnp.int32, (index.shape[0], row.shape[1]), 1)
+    return jnp.sum(jnp.where(lane == index, row, 0.0), axis=1, keepdims=True)
+
+
+def iota_col(n):
+    return lax.broadcasted_iota(jnp.int32, (n, 1), 0)
+
+
+def kernel(
+    t_hbm, v_hbm, eo_ref, ev_ref, so_ref, sv_ref, pair_ref, out_ref, over_ref,
+    t_buf, v_buf, vm, vt, tm, tt, t_send, t_recv, a_send, a_recv, blocks, weight, a_main, a_tail,
+    in_sem, ts_sem, tr_sem, as_sem, ar_sem, gs_sem, gr_sem,
+):
+    occ, vir = lax.axis_index("occ"), lax.axis_index("vir")
+    x, zl, core = occ // 4, (occ // 2) % 2, occ % 2
+
+    def member(step):
+        return ((x + step[0]) % 4) * 4 + ((zl + step[1]) % 2) * 2 + (core + step[2]) % 2
+
+    load_v = pltpu.make_async_copy(v_hbm, v_buf, in_sem.at[0])
+    load_t = pltpu.make_async_copy(t_hbm, t_buf, in_sem.at[1])
+    load_v.start()
+    load_t.start()
+
+    others = [(i // 4, (i // 2) % 2, i % 2) for i in range(1, 16)]
+    mirror_occ = vir // 2
+    mirror_self = mirror_occ == occ
+    bar = pltpu.get_barrier_semaphore()
+    for step in others:
+        pl.semaphore_signal(bar, inc=1, device_id={"occ": member(step)}, device_id_type=MESH)
+    for h in range(2):
+
+        @pl.when(jnp.logical_not(jnp.logical_and(mirror_self, vir % 2 == h)))
+        def _():
+            pl.semaphore_signal(bar, inc=1, device_id={"occ": mirror_occ, "vir": 2 * occ + h}, device_id_type=MESH)
+
+    pair = pair_ref[...]
+    hot = jnp.where(pair == lax.broadcasted_iota(jnp.int32, (8, pair.shape[1]), 0), 1.0, 0.0)
+    upper = lax.broadcasted_iota(jnp.int32, (128, 128), 0) <= lax.broadcasted_iota(jnp.int32, (128, 128), 1)
+    upper = jnp.where(upper, 1.0, 0.0).astype(BF16)
+    parts = [hot[:, 128 * c : 128 * (c + 1)] for c in range(8)]
+    counted = jnp.dot(jnp.concatenate(parts, axis=0).astype(BF16), upper, preferred_element_type=F32)
+    before = jnp.zeros((8, 1), F32)
+    ranks = []
+    for c in range(8):
+        here = counted[8 * c : 8 * (c + 1)]
+        ranks.append(jnp.sum(parts[c] * (here + before), axis=0, keepdims=True))
+        before = before + here[:, 127:128]
+    rank = jnp.concatenate(ranks, axis=1) - 1.0
+    over_ref[...] = jnp.broadcast_to(jnp.max(before, axis=0, keepdims=True), over_ref.shape).astype(jnp.int32)
+    lane_of = iota_col(2 * LANES)
+    lane_of = jnp.where(lane_of < CAP, lane_of, lane_of - TAIL).astype(F32)
+    place = jnp.where(rank == lane_of, 1.0, 0.0).astype(BF16)
+
+    sv_row = sv_ref[...].astype(F32)
+    so_row = so_ref[...].astype(F32)
+    first_half = lax.broadcasted_iota(jnp.int32, (1, LANES), 1) < TAIL
+
+    def compact(values, sym):
+        high, low = split(jnp.where(pair == sym, values, 0.0))
+        return dot_t(high, place) + dot_t(low, place)
+
+    rows = iota_col(128)
+    sym_v = at_lane(sv_row, 8 * vir + rows // 16).astype(jnp.int32) ^ at_lane(sv_row, 16 * occ + rows % 16).astype(jnp.int32)
+    load_v.wait()
+    small = compact(v_buf[...].reshape(128, 1024), sym_v)
+    vm[...] = small[:, :LANES]
+    vt[...] = small[:, LANES:]
+    for h in range(2):
+        for q in range(4):
+            for t in range(2):
+                t_send[h, 3 * q + t] = vm[pl.ds(8 * h + q + 4 * t, 8, stride=16), :]
+            t_send[h, 3 * q + 2] = jnp.where(
+                first_half, vt[pl.ds(8 * h + q, 8, stride=16), :], vt[pl.ds(8 * h + q + 4, 8, stride=16), :]
+            )
+
+    @pl.when(mirror_self)
+    def _():
+        pl.semaphore_wait(bar, 16)
+
+    @pl.when(jnp.logical_not(mirror_self))
+    def _():
+        pl.semaphore_wait(bar, 17)
+
+    def mirror(h, slot):
+        return pltpu.make_async_remote_copy(
+            src_ref=t_send.at[h],
+            dst_ref=t_recv.at[slot],
+            send_sem=ts_sem.at[h],
+            recv_sem=tr_sem.at[slot],
+            device_id={"occ": mirror_occ, "vir": 2 * occ + h},
+            device_id_type=MESH,
+        )
+
+    for h in range(2):
+        to_self = jnp.logical_and(mirror_self, vir % 2 == h)
+
+        @pl.when(to_self)
+        def _():
+            t_recv[h] = t_send[h]
+
+        @pl.when(jnp.logical_not(to_self))
+        def _():
+            mirror(h, vir % 2).start()
+
+    rows = iota_col(256)
+    sym_t = at_lane(so_row, 4 * occ + rows // 64).astype(jnp.int32) ^ at_lane(so_row, rows % 64).astype(jnp.int32)
+    load_t.wait()
+    small = compact(t_buf[...].reshape(256, 1024), sym_t)
+    tm[...] = small[:, :LANES]
+    tt[...] = small[:, LANES:]
+    for i in range(4):
+        for j in range(4):
+            a_send[pl.ds(4 * i + j, 16, stride=24), :] = tm[pl.ds(64 * i + j, 16, stride=4), :]
+        for j in range(2):
+            a_send[pl.ds(16 + 2 * i + j, 16, stride=24), :] = jnp.where(
+                first_half, tt[pl.ds(64 * i + j, 16, stride=4), :], tt[pl.ds(64 * i + j + 2, 16, stride=4), :]
+            )
+
+    def swap(n, step):
+        there = member(step)
+        return pltpu.make_async_remote_copy(
+            src_ref=a_send.at[pl.ds(pl.multiple_of(24 * there, 8), 24), :],
+            dst_ref=a_recv.at[pl.ds(pl.multiple_of(24 * occ, 8), 24), :],
+            send_sem=as_sem.at[n],
+            recv_sem=ar_sem.at[n],
+            device_id={"occ": there},
+            device_id_type=MESH,
+        )
+
+    swaps = [swap(n, step) for n, step in enumerate(others)]
+    for copy in swaps:
+        copy.start()
+    mine = pl.ds(pl.multiple_of(24 * occ, 8), 24)
+    a_recv[mine, :] = a_send[mine, :]
+
+    j_of = 4 * (rows % 16) + (rows // 16) % 4
+    sym_ij = at_lane(so_row, 4 * occ + rows // 64).astype(jnp.int32) ^ at_lane(so_row, j_of).astype(jnp.int32)
+    eo_row, ev_row = eo_ref[...], ev_ref[...]
+    e_ij = at_lane(eo_row, 4 * occ + rows // 64) + at_lane(eo_row, j_of)
+    sv_int = sv_ref[...]
+
+    def weigh(a, carry):
+        which = jnp.full((1, 1), 8 * vir + a, jnp.int32)
+        sym_b = sv_int ^ at_lane(sv_row, which).astype(jnp.int32)
+        e_b = at_lane(ev_row, which) + ev_row
+        weight[a] = jnp.where(sym_ij == sym_b, 1.0 / (e_ij - e_b), 0.0)
+        return carry
+
+    lax.fori_loop(0, 8, weigh, 0)
+
+    here = pl.multiple_of(16 * occ, 16)
+    for g in range(2):
+        from_self = jnp.logical_and(mirror_self, vir % 2 == g)
+
+        @pl.when(jnp.logical_not(from_self))
+        def _():
+            mirror(g, g).wait_recv()
+
+        for q in range(4):
+            for t in range(2):
+                own = vm[pl.ds(16 * (q + 4 * t) + 8 * g, 8), :]
+                blocks[3 * q + t, pl.ds(here + 8 * g, 8), :] = own - t_recv[g, 3 * q + t]
+            own = jnp.where(first_half, vt[pl.ds(16 * q + 8 * g, 8), :], vt[pl.ds(16 * (q + 4) + 8 * g, 8), :])
+            blocks[3 * q + 2, pl.ds(here + 8 * g, 8), :] = own - t_recv[g, 3 * q + 2]
+
+    width = 12 // CHUNKS
+
+    def hop(n):
+        chunk, whose, half, route, _ = GATHER[n]
+        first = 16 * member(whose)
+        size = 16
+        if half is not None:
+            first, size = first + 8 * half, 8
+        part = blocks.at[pl.ds(chunk * width, width), pl.ds(pl.multiple_of(first, 8), size), :]
+        return pltpu.make_async_remote_copy(
+            src_ref=part,
+            dst_ref=part,
+            send_sem=gs_sem.at[n],
+            recv_sem=gr_sem.at[n],
+            device_id={"occ": member(route)},
+            device_id_type=MESH,
+        )
+
+    def landing(n):
+        chunk, whose, half, route, _ = GATHER[n]
+        back = tuple((k - r) % m for k, r, m in zip(whose, route, (4, 2, 2)))
+        first = 16 * member(back)
+        size = 16
+        if half is not None:
+            first, size = first + 8 * half, 8
+        part = blocks.at[pl.ds(chunk * width, width), pl.ds(pl.multiple_of(first, 8), size), :]
+        return pltpu.make_async_remote_copy(
+            src_ref=part,
+            dst_ref=part,
+            send_sem=gs_sem.at[n],
+            recv_sem=gr_sem.at[n],
+            device_id={"occ": member(route)},
+            device_id_type=MESH,
+        )
+
+    arrived = set()
+
+    def need(n):
+        if n not in arrived:
+            arrived.add(n)
+            landing(n).wait_recv()
+
+    def antisymmetrize_amplitudes():
+        for n, copy in enumerate(swaps):
+            copy.wait_recv()
+        for i in range(4):
+            for j in range(4):
+                to = pl.ds(64 * i + 16 * j, 16)
+                a_main[to, :] = tm[pl.ds(64 * i + j, 16, stride=4), :] - a_recv[pl.ds(4 * j + i, 16, stride=24), :]
+                tail = a_recv[pl.ds(16 + 2 * j + i % 2, 16, stride=24), :]
+                turned = pltpu.roll(tail, TAIL, 1)
+                tail = jnp.where(first_half, tail, turned) if i < 2 else jnp.where(first_half, turned, tail)
+                a_tail[to, :] = tt[pl.ds(64 * i + j, 16, stride=4), :] - tail
+
+    prepared = []
+
+    def multiply(chunk):
+        if not prepared:
+            antisymmetrize_amplitudes()
+            main = a_main[...]
+            tail = a_tail[...]
+            for t in range(2):
+                kept = jnp.where(first_half if t == 0 else jnp.logical_not(first_half), tail, 0.0)
+                prepared.append(split(jnp.concatenate([main, kept], axis=1)))
+        for q in range(chunk * width // 3, (chunk + 1) * width // 3):
+            for t in range(2):
+                a_high, a_low = prepared[t]
+                b_high, b_low = split(jnp.concatenate([blocks[3 * q + t], blocks[3 * q + 2]], axis=1))
+                c = dot_t(a_high, b_high) + (dot_t(a_low, b_high) + dot_t(a_high, b_low))
+                c = c * weight[q + 4 * t]
+                for i in range(4):
+                    for j in range(4):
+                        part = c[64 * i + 16 * j : 64 * i + 16 * (j + 1)]
+                        for s in range(2):
+                            out_ref[s, pl.ds(8 * (64 * i + j) + q + 4 * t, 16, stride=32), :] = part[
+                                :, 128 * s : 128 * (s + 1)
+                            ]
+
+    for n, op in enumerate(GATHER):
+        for m in op[4]:
+            need(m)
+        hop(n).start()
+    for chunk in range(CHUNKS):
+        for n, op in enumerate(GATHER):
+            if op[0] == chunk:
+                need(n)
+        multiply(chunk)
+
+    for h in range(2):
+
+        @pl.when(jnp.logical_not(jnp.logical_and(mirror_self, vir % 2 == h)))
+        def _():
+            mirror(h, vir % 2).wait_send()
+
+    for copy in swaps:
+        copy.wait_send()
+    for n in range(len(GATHER)):
+        hop(n).wait_send()
+
+
+def compacted(amplitudes, integrals, occ_energy, vir_energy, occ_irrep, vir_irrep, pair_irrep):
+    whole = pl.BlockSpec(memory_space=pltpu.VMEM)
+    away = pl.BlockSpec(memory_space=pl.ANY)
+    sems = pltpu.SemaphoreType.DMA
+    out, over = pl.pallas_call(
+        kernel,
+        out_shape=(
+            jax.ShapeDtypeStruct((2, 2048, 128), F32),
+            jax.ShapeDtypeStruct((8, 128), jnp.int32),
+        ),
+        in_specs=[away, away] + [whole] * 5,
+        out_specs=(whole, whole),
+        scratch_shapes=[
+            pltpu.VMEM((4, 64, 1024), F32),
+            pltpu.VMEM((8, 16, 1024), F32),
+            pltpu.VMEM((128, LANES), F32),
+            pltpu.VMEM((128, LANES), F32),
+            pltpu.VMEM((256, LANES), F32),
+            pltpu.VMEM((256, LANES), F32),
+            pltpu.VMEM((2, 12, 8, LANES), F32),
+            pltpu.VMEM((2, 12, 8, LANES), F32),
+            pltpu.VMEM((16 * 24, LANES), F32),
+            pltpu.VMEM((16 * 24, LANES), F32),
+            pltpu.VMEM((12, 256, LANES), F32),
+            pltpu.VMEM((8, 256, 256), F32),
+            pltpu.VMEM((256, LANES), F32),
+            pltpu.VMEM((256, LANES), F32),
+            sems((2,)),
+            sems((2,)),
+            sems((2,)),
+            sems((15,)),
+            sems((15,)),
+            sems((len(GATHER),)),
+            sems((len(GATHER),)),
+        ],
+        compiler_params=pltpu.CompilerParams(collective_id=0, has_side_effects=True, vmem_limit_bytes=40 * 2**20),
+        name="ladder",
+    )(
+        amplitudes,
+        integrals,
+        occ_energy.reshape(1, -1),
+        vir_energy.reshape(1, -1),
+        occ_irrep.reshape(1, -1),
+        vir_irrep.reshape(1, -1),
+        pair_irrep.reshape(1, -1),
+    )
+    out = jnp.transpose(out.reshape(2, 4, 64, 8, 128), (1, 2, 3, 0, 4)).reshape(4, 64, 8, 256)
+    return out, over[0, 0]
+
+
+def dense(amplitudes, integrals, occ_energy, vir_energy, occ_irrep, vir_irrep, pair_irrep):
     occ_rows = amplitudes.shape[0]
     vir_rows = integrals.shape[0]
     vir_cols = integrals.shape[1]
@@ -44,6 +414,11 @@
     return anti / denom
 
 
+def local(*args):
+    out, most = compacted(*args)
+    return lax.cond(most > CAP, lambda out: dense(*args), lambda out: out, out)
+
+
 def solution(mesh):
     placed = (P("occ", None, None), P("vir", "occ", None), P(), P(), P(), P(), P())
     return jax.shard_map(

time: 250 us -> 66.7 us (0.27); the launches traced: 246 us -> 66.3 us
  waiting for transfers between devices: 130 us -> 0 us
  Pallas kernels: 0 us -> 42.9 us
  blocking collectives: 31.6 us -> 0 us
  local copies, waits for them, and re-layouts: 33.9 us -> 8.97 us
  other arithmetic: 16.1 us -> 0 us
  starting transfers between devices: 11.9 us -> 0 us
  matrix products: 9.66 us -> 0 us
    all_to_all x1 -> x0, waiting for transfers between devices: 67.2 us -> none  [local(): lax.all_to_all(occ_anti, 'vir', split_axis=3, concat_axis=2, tiled=True)]
    all_gather x1 -> x0, waiting for transfers between devices: 62.3 us -> none  [local(): lax.all_gather(masked_int, 'occ', axis=1, tiled=True)]
    pallas_call x0 -> x1, Pallas kernels: none -> 42.9 us  [compacted(): pl.pallas_call(kernel, out_shape=(jax.ShapeDtypeStruct((2, 2048, 128), F3...]
    all_to_all x1 -> x0, blocking collectives: 31.6 us -> none  [local(): lax.all_to_all(ladder, 'occ', split_axis=1, concat_axis=0, tiled=True)]
    all_to_all x5 -> x0, local copies, waits for them, and re-layouts: 13.5 us -> none  [the longest x3 10.9 us: local(): lax.all_to_all(occ_anti, 'vir', split_axis=3, concat_axis=2, tiled=True)]
    all_to_all x1 -> x0, starting transfers between devices: 11.9 us -> none  [local(): lax.all_to_all(occ_anti, 'vir', split_axis=3, concat_axis=2, tiled=True)]
    dot_general x1 -> x0, matrix products: 9.66 us -> none  [local(): jnp.einsum('ijk,abk->ijab', masked_amp, lax.all_gather(masked_int, 'occ',...]
    all_to_all x1 -> x0, other arithmetic: 8.75 us -> none  [local(): lax.all_to_all(occ_anti, 'vir', split_axis=3, concat_axis=2, tiled=True)]
  transfers between devices with their start and end apart: 2 -> 0, of which waited for: 2 -> 0; matrix products, arithmetic and copies ran while one was open for 1% -> 0% of each run, Pallas kernels for 0% -> 0%
where the time goes in v1:
time: 66.7 us; the launch traced here: 66.3 us
  Pallas kernels  42.9 us (64%)
  between operations  14.2 us (21%)
  local copies, waits for them, and re-layouts  8.97 us (13%)
    pallas_call x1, Pallas kernels, compacted(): pl.pallas_call(kernel, out_shape=(jax.ShapeDtypeStruct((2, 2048, 128), F3...  42.9 us
    cond x1, local copies, waits for them, and re-layouts  2.81 us
    reshape x1, local copies, waits for them, and re-layouts, compacted(): jnp.transpose(out.reshape(2, 4, 64, 8, 128), (1, 2, 3, 0, 4))  2.68 us
    reshape x1, local copies, waits for them, and re-layouts, compacted(): out.reshape(2, 4, 64, 8, 128)  1.62 us
    unnamed x14, local copies, waits for them, and re-layouts  1.35 us

profile of v1, /device:TPU:1, one launch (start us, length us, event | category | flops | bytes accessed | tf_op | source)
XLA Modules:
  0.0 66.3 jit_solution(13114950312076932143)
XLA Ops:
  6.5 42.9 %ladder.1 = (f32[2,2048,128]{2,1,0:T(8,128)S(1)}, s32[8,128]{1,0:T(8,128)S(1)}) custom-call(f32[4,64,1024]{2,1,0:T(8,128)} %t_hbm.1, f32[8,16,1024]{2,1,0:T(8,128)} %v_hbm.1, f32[1,64]{1,0:T(1,128)} %bitcast.47, f32[1,256]{1,0:T(1,128)} %bitcast.46, s32[1,64]{1,0:T(1,128)} %bitcast.48, s32[1,256]{1,0:T(1,128)} %bitcast.49, s32[1,1024]{1,0:T(1,128)} %bitcast.45), custom_call_target="tpu_custom_call" | custom-call | tf_op jit(solution)/shard_map/ladder/pallas_call | solution.py:331
  49.4 0.0 copy-start.1
  49.5 0.0 copy-start.3
  49.5 0.0 copy-start.4
  49.5 0.0 copy-start.5
  49.5 0.0 copy-start.6
  49.5 0.0 copy-start.7
  49.5 1.6 %copy.35 = f32[2,4,64,8,128]{4,0,2,3,1:T(2,128)S(1)} copy(f32[2,4,64,8,128]{4,3,2,1,0:T(8,128)S(1)} %bitcast.38) | data formatting | bytes 4194304 | tf_op jit(solution)/shard_map/reshape | solution.py:373
  51.1 0.5 slice.3
  52.3 0.0 copy-done.1
  52.3 0.0 copy-done.3
  52.3 0.0 copy-done.4
  52.3 0.0 copy-done.5
  52.4 0.0 copy-done.6
  52.4 0.0 copy-done.7
  52.4 5.7 %conditional.1 = (f32[4,64,8,256]{3,2,1,0:T(8,128)S(1)}) conditional(s32[]{:T(128)} %bitcast.16, f32[4,64,8,2,128]{4,3,1,2,0:T(2,128)S(1)} %bitcast.42, (s32[64]{0:T(128)S(1)}, s32[1024]{0:T(1024)S(1)}, f32[4,64,1024]{2,1,0:T(8,128)S(1)}, s32[256]{0:T(256)S(1)}, f32[8,16,1024]{2,1,0:T(8,128)}, /*index=5*/f32[64]{0:T(128)S(1)}, f32[256]{0:T(256)S(1)}) %tuple.27), branch_computations={%region_0.0_spmd, %region_1.2_spmd} | conditional | flops 6445337600 | bytes 112753960 | solution.py:419
  52.4 2.7 %reshape.116 = f32[4,64,8,256]{3,1,2,0:T(8,128)} reshape(f32[4,64,8,2,128]{4,3,1,2,0:T(2,128)S(1)} %param) | data formatting | bytes 4194304 | tf_op jit(solution)/shard_map/reshape | solution.py:373
  55.1 2.8 %copy.30 = f32[4,64,8,256]{3,2,1,0:T(8,128)S(1)} copy(f32[4,64,8,256]{3,1,2,0:T(8,128)} %reshape.116) | data formatting | bytes 4194304 | tf_op jit(solution)/shard_map/cond
  58.1 0.0 copy-start.2
  58.1 1.3 %copy-done.2 = f32[4,64,8,256]{3,2,1,0:T(8,128)} copy-done((f32[4,64,8,256]{3,2,1,0:T(8,128)}, f32[4,64,8,256]{3,2,1,0:T(8,128)S(1)}, u32[]{:S(2)}) %copy-start.2) | copy-done | bytes 2097176
Async XLA Ops:
  49.4 2.9 %copy-start.1 = (f32[4,64,1024]{2,1,0:T(8,128)S(1)}, f32[4,64,1024]{2,1,0:T(8,128)}, u32[]{:S(2)}) copy-start(f32[4,64,1024]{2,1,0:T(8,128)} %t_hbm.1) | copy-start | bytes 3145732
  49.5 2.9 %copy-start.3 = (s32[1024]{0:T(1024)S(1)}, s32[1024]{0:T(1024)}, u32[]{:S(2)}) copy-start(s32[1024]{0:T(1024)} %param.15) | copy-start | bytes 12292
  49.5 2.9 %copy-start.4 = (f32[256]{0:T(256)S(1)}, f32[256]{0:T(256)}, u32[]{:S(2)}) copy-start(f32[256]{0:T(256)} %param.12) | copy-start | bytes 3076
  49.5 2.9 %copy-start.5 = (f32[64]{0:T(128)S(1)}, f32[64]{0:T(128)}, u32[]{:S(2)}) copy-start(f32[64]{0:T(128)} %param.11) | copy-start | bytes 772
  49.5 2.9 %copy-start.6 = (s32[64]{0:T(128)S(1)}, s32[64]{0:T(128)}, u32[]{:S(2)}) copy-start(s32[64]{0:T(128)} %param.13) | copy-start | bytes 772
  49.5 2.9 %copy-start.7 = (s32[256]{0:T(256)S(1)}, s32[256]{0:T(256)}, u32[]{:S(2)}) copy-start(s32[256]{0:T(256)} %param.14) | copy-start | bytes 3076
  58.1 1.3 %copy-start.2 = (f32[4,64,8,256]{3,2,1,0:T(8,128)}, f32[4,64,8,256]{3,2,1,0:T(8,128)S(1)}, u32[]{:S(2)}) copy-start(f32[4,64,8,256]{3,2,1,0:T(8,128)S(1)} %get-tuple-element.44) | copy-start | bytes 6291460

commit v2 on v1

--- a/solution.py
+++ b/solution.py
@@ -16,14 +16,11 @@
 CAP = LANES + TAIL
 CHUNKS = 2
 
-OWN, XP, XM, X2 = (0, 0, 0), (1, 0, 0), (3, 0, 0), (2, 0, 0)
-Z, ZP, ZM, Z2 = (0, 1, 0), (1, 1, 0), (3, 1, 0), (2, 1, 0)
-CORE = (0, 0, 1)
+OWN, CORE = (0, 0, 0), (0, 0, 1)
+SAME = ((2, 1, 0), (2, 0, 0), (1, 1, 0), (3, 1, 0), (1, 0, 0), (3, 0, 0), (0, 1, 0))
 STAGES = (
-    ((OWN, None, Z), (OWN, None, XP), (OWN, None, XM), (OWN, None, CORE)),
-    ((Z, None, XP), (Z, None, XM), (XM, 0, XP), (XP, 1, XM), (Z, None, CORE), (XM, None, CORE), (XP, None, CORE)),
-    ((X2, 0, Z), (X2, 1, Z), (X2, 0, CORE), (X2, 1, CORE), (ZM, None, CORE), (ZP, None, CORE)),
-    ((Z2, 0, CORE), (Z2, 1, CORE)),
+    tuple((OWN, step) for step in SAME) + ((OWN, CORE),),
+    tuple((((-step[0]) % 4, step[1], 0), CORE) for step in reversed(SAME)),
 )
 
 
@@ -33,15 +30,11 @@
         for chunk in range(CHUNKS):
             if not 0 <= tick - chunk < len(STAGES):
                 continue
-            for whose, half, route in STAGES[tick - chunk]:
+            for whose, route in STAGES[tick - chunk]:
                 there = tuple((k - r) % n for k, r, n in zip(whose, route, (4, 2, 2)))
-                after = []
-                if whose != OWN:
-                    for h in (0, 1, None):
-                        if (chunk, whose, h) in arrived and (half is None or h is None or h == half):
-                            after.append(arrived[chunk, whose, h])
-                arrived[chunk, there, half] = len(ops)
-                ops.append((chunk, whose, half, route, tuple(after)))
+                after = arrived[chunk, whose] if whose != OWN else None
+                arrived[chunk, there] = len(ops)
+                ops.append((chunk, whose, route, after))
     return ops
 
 
@@ -67,7 +60,7 @@
 
 
 def kernel(
-    t_hbm, v_hbm, eo_ref, ev_ref, so_ref, sv_ref, pair_ref, out_ref, over_ref,
+    t_hbm, v_hbm, eo_ref, ev_ref, so_ref, sv_ref, pair_ref, turn_ref, out_ref, most_ref,
     t_buf, v_buf, vm, vt, tm, tt, t_send, t_recv, a_send, a_recv, blocks, weight, a_main, a_tail,
     in_sem, ts_sem, tr_sem, as_sem, ar_sem, gs_sem, gr_sem,
 ):
@@ -106,8 +99,8 @@
         here = counted[8 * c : 8 * (c + 1)]
         ranks.append(jnp.sum(parts[c] * (here + before), axis=0, keepdims=True))
         before = before + here[:, 127:128]
-    rank = jnp.concatenate(ranks, axis=1) - 1.0
-    over_ref[...] = jnp.broadcast_to(jnp.max(before, axis=0, keepdims=True), over_ref.shape).astype(jnp.int32)
+    rank = jnp.concatenate(ranks, axis=1) - 1.0 - CAP * turn_ref[...].astype(F32)
+    most_ref[...] = jnp.broadcast_to(jnp.max(before, axis=0, keepdims=True), most_ref.shape).astype(jnp.int32)
     lane_of = iota_col(2 * LANES)
     lane_of = jnp.where(lane_of < CAP, lane_of, lane_of - TAIL).astype(F32)
     place = jnp.where(rank == lane_of, 1.0, 0.0).astype(BF16)
@@ -194,17 +187,15 @@
     mine = pl.ds(pl.multiple_of(24 * occ, 8), 24)
     a_recv[mine, :] = a_send[mine, :]
 
-    j_of = 4 * (rows % 16) + (rows // 16) % 4
-    sym_ij = at_lane(so_row, 4 * occ + rows // 64).astype(jnp.int32) ^ at_lane(so_row, j_of).astype(jnp.int32)
     eo_row, ev_row = eo_ref[...], ev_ref[...]
-    e_ij = at_lane(eo_row, 4 * occ + rows // 64) + at_lane(eo_row, j_of)
+    e_ij = at_lane(eo_row, 4 * occ + rows // 64) + at_lane(eo_row, rows % 64)
     sv_int = sv_ref[...]
 
     def weigh(a, carry):
         which = jnp.full((1, 1), 8 * vir + a, jnp.int32)
         sym_b = sv_int ^ at_lane(sv_row, which).astype(jnp.int32)
         e_b = at_lane(ev_row, which) + ev_row
-        weight[a] = jnp.where(sym_ij == sym_b, 1.0 / (e_ij - e_b), 0.0)
+        weight[a] = jnp.where(sym_t == sym_b, 1.0 / (e_ij - e_b), 0.0)
         return carry
 
     lax.fori_loop(0, 8, weigh, 0)
@@ -226,13 +217,11 @@
 
     width = 12 // CHUNKS
 
-    def hop(n):
-        chunk, whose, half, route, _ = GATHER[n]
-        first = 16 * member(whose)
-        size = 16
-        if half is not None:
-            first, size = first + 8 * half, 8
-        part = blocks.at[pl.ds(chunk * width, width), pl.ds(pl.multiple_of(first, 8), size), :]
+    def hop(n, landing=False):
+        chunk, whose, route, _ = GATHER[n]
+        if landing:
+            whose = tuple((k - r) % m for k, r, m in zip(whose, route, (4, 2, 2)))
+        part = blocks.at[pl.ds(chunk * width, width), pl.ds(pl.multiple_of(16 * member(whose), 16), 16), :]
         return pltpu.make_async_remote_copy(
             src_ref=part,
             dst_ref=part,
@@ -242,41 +231,24 @@
             device_id_type=MESH,
         )
 
-    def landing(n):
-        chunk, whose, half, route, _ = GATHER[n]
-        back = tuple((k - r) % m for k, r, m in zip(whose, route, (4, 2, 2)))
-        first = 16 * member(back)
-        size = 16
-        if half is not None:
-            first, size = first + 8 * half, 8
-        part = blocks.at[pl.ds(chunk * width, width), pl.ds(pl.multiple_of(first, 8), size), :]
-        return pltpu.make_async_remote_copy(
-            src_ref=part,
-            dst_ref=part,
-            send_sem=gs_sem.at[n],
-            recv_sem=gr_sem.at[n],
-            device_id={"occ": member(route)},
-            device_id_type=MESH,
-        )
-
     arrived = set()
 
     def need(n):
         if n not in arrived:
             arrived.add(n)
-            landing(n).wait_recv()
+            hop(n, landing=True).wait_recv()
 
     def antisymmetrize_amplitudes():
         for n, copy in enumerate(swaps):
             copy.wait_recv()
         for i in range(4):
             for j in range(4):
-                to = pl.ds(64 * i + 16 * j, 16)
-                a_main[to, :] = tm[pl.ds(64 * i + j, 16, stride=4), :] - a_recv[pl.ds(4 * j + i, 16, stride=24), :]
+                to = pl.ds(64 * i + j, 16, stride=4)
+                a_main[to, :] = tm[to, :] - a_recv[pl.ds(4 * j + i, 16, stride=24), :]
                 tail = a_recv[pl.ds(16 + 2 * j + i % 2, 16, stride=24), :]
                 turned = pltpu.roll(tail, TAIL, 1)
                 tail = jnp.where(first_half, tail, turned) if i < 2 else jnp.where(first_half, turned, tail)
-                a_tail[to, :] = tt[pl.ds(64 * i + j, 16, stride=4), :] - tail
+                a_tail[to, :] = tt[to, :] - tail
 
     prepared = []
 
@@ -293,18 +265,11 @@
                 a_high, a_low = prepared[t]
                 b_high, b_low = split(jnp.concatenate([blocks[3 * q + t], blocks[3 * q + 2]], axis=1))
                 c = dot_t(a_high, b_high) + (dot_t(a_low, b_high) + dot_t(a_high, b_low))
-                c = c * weight[q + 4 * t]
-                for i in range(4):
-                    for j in range(4):
-                        part = c[64 * i + 16 * j : 64 * i + 16 * (j + 1)]
-                        for s in range(2):
-                            out_ref[s, pl.ds(8 * (64 * i + j) + q + 4 * t, 16, stride=32), :] = part[
-                                :, 128 * s : 128 * (s + 1)
-                            ]
+                out_ref[q + 4 * t] = c * weight[q + 4 * t]
 
     for n, op in enumerate(GATHER):
-        for m in op[4]:
-            need(m)
+        if op[3] is not None:
+            need(op[3])
         hop(n).start()
     for chunk in range(CHUNKS):
         for n, op in enumerate(GATHER):
@@ -324,17 +289,17 @@
         hop(n).wait_send()
 
 
-def compacted(amplitudes, integrals, occ_energy, vir_energy, occ_irrep, vir_irrep, pair_irrep):
+def one_pass(turn, amplitudes, integrals, occ_energy, vir_energy, occ_irrep, vir_irrep, pair_irrep):
     whole = pl.BlockSpec(memory_space=pltpu.VMEM)
     away = pl.BlockSpec(memory_space=pl.ANY)
     sems = pltpu.SemaphoreType.DMA
-    out, over = pl.pallas_call(
+    out, most = pl.pallas_call(
         kernel,
         out_shape=(
-            jax.ShapeDtypeStruct((2, 2048, 128), F32),
-            jax.ShapeDtypeStruct((8, 128), jnp.int32),
+            jax.ShapeDtypeStruct((8, 256, 256), F32),
+            jax.ShapeDtypeStruct((1, 1), jnp.int32),
         ),
-        in_specs=[away, away] + [whole] * 5,
+        in_specs=[away, away] + [whole] * 6,
         out_specs=(whole, whole),
         scratch_shapes=[
             pltpu.VMEM((4, 64, 1024), F32),
@@ -369,54 +334,24 @@
         occ_irrep.reshape(1, -1),
         vir_irrep.reshape(1, -1),
         pair_irrep.reshape(1, -1),
+        turn,
     )
-    out = jnp.transpose(out.reshape(2, 4, 64, 8, 128), (1, 2, 3, 0, 4)).reshape(4, 64, 8, 256)
-    return out, over[0, 0]
-
-
-def dense(amplitudes, integrals, occ_energy, vir_energy, occ_irrep, vir_irrep, pair_irrep):
-    occ_rows = amplitudes.shape[0]
-    vir_rows = integrals.shape[0]
-    vir_cols = integrals.shape[1]
-    occ_start = lax.axis_index("occ") * occ_rows
-    vir_start = lax.axis_index("vir") * vir_rows
-    col_start = lax.axis_index("occ") * vir_cols
-    own_occ = lax.dynamic_slice_in_dim(occ_irrep, occ_start, occ_rows)
-    pair_sym = jnp.bitwise_xor(own_occ[:, None], occ_irrep[None, :])
-    masked_amp = jnp.where(
-        pair_sym[:, :, None] == pair_irrep[None, None, :], amplitudes, jnp.float32(0.0)
-    )
-    own_vir = lax.dynamic_slice_in_dim(vir_irrep, vir_start, vir_rows)
-    col_vir = lax.dynamic_slice_in_dim(vir_irrep, col_start, vir_cols)
-    vir_sym = jnp.bitwise_xor(own_vir[:, None], col_vir[None, :])
-    masked_int = jnp.where(
-        vir_sym[:, :, None] == pair_irrep[None, None, :], integrals, jnp.float32(0.0)
-    )
-    ladder = jnp.einsum(
-        "ijk,abk->ijab",
-        masked_amp,
-        lax.all_gather(masked_int, "occ", axis=1, tiled=True),
-        precision=lax.Precision.HIGHEST,
-        preferred_element_type=jnp.float32,
-    )
-    ladder_swap = lax.all_to_all(ladder, "occ", split_axis=1, concat_axis=0, tiled=True)
-    occ_anti = ladder - jnp.transpose(ladder_swap, (1, 0, 2, 3))
-    virt_swap = lax.all_to_all(occ_anti, "vir", split_axis=3, concat_axis=2, tiled=True)
-    anti = occ_anti - jnp.transpose(virt_swap, (0, 1, 3, 2))
-    own_occ_energy = lax.dynamic_slice_in_dim(occ_energy, occ_start, occ_rows)
-    own_vir_energy = lax.dynamic_slice_in_dim(vir_energy, vir_start, vir_rows)
-    denom = (
-        own_occ_energy[:, None, None, None]
-        + occ_energy[None, :, None, None]
-        - own_vir_energy[None, None, :, None]
-        - vir_energy[None, None, None, :]
-    )
-    return anti / denom
+    return out, most
 
 
 def local(*args):
-    out, most = compacted(*args)
-    return lax.cond(most > CAP, lambda out: dense(*args), lambda out: out, out)
+    turn = jnp.zeros((1, 1), jnp.int32)
+    out, most = one_pass(turn, *args)
+
+    def more(state):
+        return (CAP * (state[0] + 1) < most)[0, 0]
+
+    def step(state):
+        turn = state[0] + 1
+        return turn, state[1] + one_pass(turn, *args)[0]
+
+    _, out = lax.while_loop(more, step, (turn, out))
+    return jnp.transpose(out.reshape(8, 4, 64, 256), (1, 2, 0, 3))
 
 
 def solution(mesh):

time: 66.7 us -> 44 us (0.66)
  between operations: 14.2 us -> 0.02 us
  local copies, waits for them, and re-layouts: 8.97 us -> 2.54 us
  Pallas kernels: 42.9 us -> 40.7 us
    reshape x2 -> x0, local copies, waits for them, and re-layouts: 4.3 us -> none  [the longest x1 2.68 us: compacted(): jnp.transpose(out.reshape(2, 4, 64, 8, 128), (1, 2, 3, 0, 4))]
    cond x1 -> x0, local copies, waits for them, and re-layouts: 2.81 us -> none
    while x0 -> x1, local copies, waits for them, and re-layouts: none -> 2.54 us  [local(): _, out = lax.while_loop(more, step, (turn, out))]
    pallas_call x1, Pallas kernels: 42.9 us -> 40.7 us  [one_pass(): pl.pallas_call(kernel, out_shape=(jax.ShapeDtypeStruct((8, 256, 256), F32...]
    unnamed x14 -> x0, local copies, waits for them, and re-layouts: 1.35 us -> none
where the time goes in v2:
time: 44 us; the launch traced here: 43.9 us
  Pallas kernels  40.7 us (93%)
  local copies, waits for them, and re-layouts  2.54 us (6%)
  loops' own time  0.64 us (1%)
    pallas_call x1, Pallas kernels, one_pass(): pl.pallas_call(kernel, out_shape=(jax.ShapeDtypeStruct((8, 256, 256), F32...  40.7 us
    while x1, local copies, waits for them, and re-layouts, local(): _, out = lax.while_loop(more, step, (turn, out))  2.54 us

profile of v2, /device:TPU:1, one launch (start us, length us, event | category | flops | bytes accessed | tf_op | source)
XLA Modules:
  0.0 43.9 jit_solution(4745547499247236007)
XLA Ops:
  0.0 40.7 %ladder.2 = (f32[8,256,256]{2,1,0:T(8,128)S(1)}, s32[1,1]{1,0:T(1,128)}) custom-call(f32[4,64,1024]{2,1,0:T(8,128)} %t_hbm.1, f32[8,16,1024]{2,1,0:T(8,128)} %v_hbm.1, f32[1,64]{1,0:T(1,128)} %bitcast.26, f32[1,256]{1,0:T(1,128)} %bitcast.22, s32[1,64]{1,0:T(1,128)} %bitcast.28, s32[1,256]{1,0:T(1,128)} %bitcast.24, s32[1,1024]{1,0:T(1,128)} %bitcast.20, ...), custom_call_target="tpu_custom_call" | custom-call | tf_op jit(solution)/shard_map/ladder/pallas_call | solution.py:296
  40.7 0.6 %while.10 = (s32[1,1]{1,0:T(1,128)}, f32[8,256,256]{2,1,0:T(8,128)S(1)}, s32[1,1]{1,0:T(1,128)}, f32[64]{0:T(128)}, f32[256]{0:T(256)}, /*index=5*/s32[64]{0:T(1...) while((s32[1,1]{1,0:T(1,128)}, ...), condition=%wide.region_1.0_spmd, body=%wide.region_0.0_spmd | while | flops 524292 | bytes 6291589 | solution.py:353
  41.3 2.5 %copy.8 = f32[8,256,256]{2,0,1:T(8,128)} copy(f32[8,256,256]{2,1,0:T(8,128)S(1)} %get-tuple-element.63) | data formatting | bytes 4194304 | tf_op jit(solution)/shard_map/while | solution.py:353

commit v3 on v2

v3 whole, which is shorter than its diff:
```python
import functools

import jax
import jax.numpy as jnp
from jax import lax
from jax.experimental import pallas as pl
from jax.experimental.pallas import tpu as pltpu
from jax.sharding import PartitionSpec as P

MESH = pl.DeviceIdType.MESH
F32 = jnp.float32
BF16 = jnp.bfloat16

LANES = 128
TAIL = 64
CAP = LANES + TAIL

OWN, XP, XM, X2 = (0, 0, 0), (1, 0, 0), (3, 0, 0), (2, 0, 0)
Z, ZP, ZM, Z2 = (0, 1, 0), (1, 1, 0), (3, 1, 0), (2, 1, 0)
CORE = (0, 0, 1)
CHIPS = (Z2, X2, ZP, ZM, XP, XM, Z)
ROUTES = (
    (OWN, X2), (OWN, Z), (OWN, XP), (OWN, XM), (OWN, CORE),
    (Z, XP), (Z, XM), (Z, CORE),
    (X2, Z), (X2, CORE),
    (XP, CORE), (XM, CORE), (ZM, CORE), (ZP, CORE), (Z2, CORE),
)


def gather_ops():
    ops, arrived = [], {}
    for whose, route in ROUTES:
        there = tuple((k - r) % n for k, r, n in zip(whose, route, (4, 2, 2)))
        after = arrived[whose] if whose != OWN else None
        arrived[there] = len(ops)
        ops.append((whose, route, after))
    return ops


GATHER = gather_ops()


def split(x):
    high = x.astype(BF16)
    return high, (x - high.astype(F32)).astype(BF16)


def dot_t(a, b):
    return lax.dot_general(a, b, (((1,), (1,)), ((), ())), preferred_element_type=F32)


def at_lane(row, index):
    lane = lax.broadcasted_iota(jnp.int32, (index.shape[0], row.shape[1]), 1)
    return jnp.sum(jnp.where(lane == index, row, 0.0), axis=1, keepdims=True)


def iota_col(n):
    return lax.broadcasted_iota(jnp.int32, (n, 1), 0)


def kernel(
    t_hbm, v_hbm, eo_hbm, ev_hbm, so_hbm, sv_hbm, pair_hbm, turn_hbm, out_ref, most_ref,
    t_buf, v_buf, eo_ref, ev_ref, so_ref, sv_ref, pair_ref, turn_ref, vm, vt, tm, tt, t_send, t_recv, a_send, a_pair, a_recv,
    blocks, weight, a_main, a_tail, in_sem, ts_sem, tr_sem, as_sem, ar_sem, gs_sem, gr_sem,
):
    occ, vir = lax.axis_index("occ"), lax.axis_index("vir")
    x, zl, core = occ // 4, (occ // 2) % 2, occ % 2

    def member(step):
        return ((x + step[0]) % 4) * 4 + ((zl + step[1]) % 2) * 2 + (core + step[2]) % 2

    mirror_occ = vir // 2
    mirror_self = mirror_occ == occ
    bar = pltpu.get_barrier_semaphore()
    for h in range(2):

        @pl.when(jnp.logical_not(jnp.logical_and(mirror_self, vir % 2 == h)))
        def _():
            pl.semaphore_signal(bar, inc=1, device_id={"occ": mirror_occ, "vir": 2 * occ + h}, device_id_type=MESH)

    for step in CHIPS + (CORE,):
        pl.semaphore_signal(bar, inc=1, device_id={"occ": member(step)}, device_id_type=MESH)

    loads = [
        pltpu.make_async_copy(src, dst, in_sem.at[n])
        for n, (src, dst) in enumerate(
            (
                (pair_hbm, pair_ref), (turn_hbm, turn_ref), (sv_hbm, sv_ref), (v_hbm, v_buf),
                (so_hbm, so_ref), (t_hbm, t_buf), (eo_hbm, eo_ref), (ev_hbm, ev_ref),
            )
        )
    ]
    for load in loads:
        load.start()
    loads[0].wait()
    loads[1].wait()

    pair = pair_ref[...]
    hot = jnp.where(pair == lax.broadcasted_iota(jnp.int32, (8, pair.shape[1]), 0), 1.0, 0.0)
    upper = lax.broadcasted_iota(jnp.int32, (128, 128), 0) <= lax.broadcasted_iota(jnp.int32, (128, 128), 1)
    upper = jnp.where(upper, 1.0, 0.0).astype(BF16)
    parts = [hot[:, 128 * c : 128 * (c + 1)] for c in range(8)]
    counted = jnp.dot(jnp.concatenate(parts, axis=0).astype(BF16), upper, preferred_element_type=F32)
    before = jnp.zeros((8, 1), F32)
    ranks = []
    for c in range(8):
        here = counted[8 * c : 8 * (c + 1)]
        ranks.append(jnp.sum(parts[c] * (here + before), axis=0, keepdims=True))
        before = before + here[:, 127:128]
    rank = jnp.concatenate(ranks, axis=1) - 1.0 - CAP * turn_ref[...].astype(F32)
    most_ref[...] = jnp.broadcast_to(jnp.max(before, axis=0, keepdims=True), most_ref.shape).astype(jnp.int32)
    lane_of = iota_col(2 * LANES)
    lane_of = jnp.where(lane_of < CAP, lane_of, lane_of - TAIL).astype(F32)
    place = jnp.where(rank == lane_of, 1.0, 0.0).astype(BF16)

    first_half = lax.broadcasted_iota(jnp.int32, (1, LANES), 1) < TAIL

    def compact(values, sym):
        high, low = split(jnp.where(pair == sym, values, 0.0))
        return dot_t(high, place) + dot_t(low, place)

    loads[2].wait()
    sv_row = sv_ref[...].astype(F32)
    rows = iota_col(128)
    sym_v = at_lane(sv_row, 8 * vir + rows // 16).astype(jnp.int32) ^ at_lane(sv_row, 16 * occ + rows % 16).astype(jnp.int32)
    loads[3].wait()
    small = compact(v_buf[...].reshape(128, 1024), sym_v)
    vm[...] = small[:, :LANES]
    vt[...] = small[:, LANES:]
    for h in range(2):
        for q in range(4):
            for t in range(2):
                t_send[h, 3 * q + t] = vm[pl.ds(8 * h + q + 4 * t, 8, stride=16), :]
            t_send[h, 3 * q + 2] = jnp.where(
                first_half, vt[pl.ds(8 * h + q, 8, stride=16), :], vt[pl.ds(8 * h + q + 4, 8, stride=16), :]
            )

    @pl.when(mirror_self)
    def _():
        pl.semaphore_wait(bar, 9)

    @pl.when(jnp.logical_not(mirror_self))
    def _():
        pl.semaphore_wait(bar, 10)

    def mirror(h, slot):
        return pltpu.make_async_remote_copy(
            src_ref=t_send.at[h],
            dst_ref=t_recv.at[slot],
            send_sem=ts_sem.at[h],
            recv_sem=tr_sem.at[slot],
            device_id={"occ": mirror_occ, "vir": 2 * occ + h},
            device_id_type=MESH,
        )

    for h in range(2):
        to_self = jnp.logical_and(mirror_self, vir % 2 == h)

        @pl.when(to_self)
        def _():
            t_recv[h] = t_send[h]

        @pl.when(jnp.logical_not(to_self))
        def _():
            mirror(h, vir % 2).start()

    loads[4].wait()
    so_row = so_ref[...].astype(F32)
    rows = iota_col(256)
    sym_t = at_lane(so_row, 4 * occ + rows // 64).astype(jnp.int32) ^ at_lane(so_row, rows % 64).astype(jnp.int32)
    loads[5].wait()
    small = compact(t_buf[...].reshape(256, 1024), sym_t)
    tm[...] = small[:, :LANES]
    tt[...] = small[:, LANES:]
    packed = a_send.reshape(2 * 8 * 24, LANES)
    for i in range(4):
        for j in range(4):
            for c in range(2):
                packed[pl.ds(192 * c + 4 * i + j, 8, stride=24), :] = tm[pl.ds(64 * i + 4 * c + j, 8, stride=8), :]
        for j in range(2):
            for c in range(2):
                packed[pl.ds(192 * c + 16 + 2 * i + j, 8, stride=24), :] = jnp.where(
                    first_half,
                    tt[pl.ds(64 * i + 4 * c + j, 8, stride=8), :],
                    tt[pl.ds(64 * i + 4 * c + j + 2, 8, stride=8), :],
                )

    chip = occ // 2
    share = pltpu.make_async_remote_copy(
        src_ref=a_send.at[1 - core],
        dst_ref=a_pair.at[:, core],
        send_sem=as_sem.at[7],
        recv_sem=ar_sem.at[7],
        device_id={"occ": member(CORE)},
        device_id_type=MESH,
    )
    share.start()
    a_pair[:, core] = a_send[core]

    def swap(n, step):
        return pltpu.make_async_remote_copy(
            src_ref=a_pair.at[member(step) // 2],
            dst_ref=a_recv.at[chip],
            send_sem=as_sem.at[n],
            recv_sem=ar_sem.at[n],
            device_id={"occ": member(step)},
            device_id_type=MESH,
        )

    loads[6].wait()
    loads[7].wait()
    eo_row, ev_row = eo_ref[...], ev_ref[...]
    e_ij = at_lane(eo_row, 4 * occ + rows // 64) + at_lane(eo_row, rows % 64)
    sv_int = sv_ref[...]

    def weigh(a, carry):
        which = jnp.full((1, 1), 8 * vir + a, jnp.int32)
        sym_b = sv_int ^ at_lane(sv_row, which).astype(jnp.int32)
        e_b = at_lane(ev_row, which) + ev_row
        weight[a] = jnp.where(sym_t == sym_b, 1.0 / (e_ij - e_b), 0.0)
        return carry

    lax.fori_loop(0, 4, weigh, 0)
    share.wait_recv()
    swaps = [swap(n, step) for n, step in enumerate(CHIPS)]
    for copy in swaps:
        copy.start()
    a_recv[chip] = a_pair[chip]
    lax.fori_loop(4, 8, weigh, 0)

    here = pl.multiple_of(16 * occ, 16)
    for g in range(2):
        from_self = jnp.logical_and(mirror_self, vir % 2 == g)

        @pl.when(jnp.logical_not(from_self))
        def _():
            mirror(g, g).wait_recv()

        for q in range(4):
            for t in range(2):
                own = vm[pl.ds(16 * (q + 4 * t) + 8 * g, 8), :]
                blocks[3 * q + t, pl.ds(here + 8 * g, 8), :] = own - t_recv[g, 3 * q + t]
            own = jnp.where(first_half, vt[pl.ds(16 * q + 8 * g, 8), :], vt[pl.ds(16 * (q + 4) + 8 * g, 8), :])
            blocks[3 * q + 2, pl.ds(here + 8 * g, 8), :] = own - t_recv[g, 3 * q + 2]

    def hop(n, landing=False):
        whose, route, _ = GATHER[n]
        if landing:
            whose = tuple((k - r) % m for k, r, m in zip(whose, route, (4, 2, 2)))
        part = blocks.at[:, pl.ds(pl.multiple_of(16 * member(whose), 16), 16), :]
        return pltpu.make_async_remote_copy(
            src_ref=part,
            dst_ref=part,
            send_sem=gs_sem.at[n],
            recv_sem=gr_sem.at[n],
            device_id={"occ": member(route)},
            device_id_type=MESH,
        )

    arrived = set()

    def need(n):
        if n not in arrived:
            arrived.add(n)
            hop(n, landing=True).wait_recv()

    for n, (_, _, after) in enumerate(GATHER):
        if after is None:
            hop(n).start()

    for copy in swaps:
        copy.wait_recv()
    theirs = a_recv.reshape(16 * 24, LANES)
    for i in range(4):
        for j in range(4):
            to = pl.ds(64 * i + j, 16, stride=4)
            a_main[to, :] = tm[to, :] - theirs[pl.ds(4 * j + i, 16, stride=24), :]
            tail = theirs[pl.ds(16 + 2 * j + i % 2, 16, stride=24), :]
            turned = pltpu.roll(tail, TAIL, 1)
            tail = jnp.where(first_half, tail, turned) if i < 2 else jnp.where(first_half, turned, tail)
            a_tail[to, :] = tt[to, :] - tail
    factors = []
    for t in range(2):
        kept = jnp.where(first_half if t == 0 else jnp.logical_not(first_half), a_tail[...], 0.0)
        high, low = split(jnp.concatenate([a_main[...], kept], axis=1))
        factors.append(jnp.concatenate([high, low, high], axis=1))

    for n, (_, _, after) in enumerate(GATHER):
        if after is not None:
            need(after)
            hop(n).start()
    for n in range(len(GATHER)):
        need(n)

    for q in range(4):
        for t in range(2):
            high, low = split(jnp.concatenate([blocks[3 * q + t], blocks[3 * q + 2]], axis=1))
            c = dot_t(factors[t], jnp.concatenate([high, high, low], axis=1))
            out_ref[q + 4 * t] = c * weight[q + 4 * t]

    for h in range(2):

        @pl.when(jnp.logical_not(jnp.logical_and(mirror_self, vir % 2 == h)))
        def _():
            mirror(h, vir % 2).wait_send()

    share.wait_send()
    for copy in swaps:
        copy.wait_send()
    for n in range(len(GATHER)):
        hop(n).wait_send()


def one_pass(turn, amplitudes, integrals, occ_energy, vir_energy, occ_irrep, vir_irrep, pair_irrep):
    whole = pl.BlockSpec(memory_space=pltpu.VMEM)
    away = pl.BlockSpec(memory_space=pl.ANY)
    sems = pltpu.SemaphoreType.DMA
    out, most = pl.pallas_call(
        kernel,
        out_shape=(
            jax.ShapeDtypeStruct((8, 256, 256), F32),
            jax.ShapeDtypeStruct((1, 1), jnp.int32),
        ),
        in_specs=[away] * 8,
        out_specs=(whole, whole),
        scratch_shapes=[
            pltpu.VMEM((4, 64, 1024), F32),
            pltpu.VMEM((8, 16, 1024), F32),
            pltpu.VMEM((1, 64), F32),
            pltpu.VMEM((1, 256), F32),
            pltpu.VMEM((1, 64), jnp.int32),
            pltpu.VMEM((1, 256), jnp.int32),
            pltpu.VMEM((1, 1024), jnp.int32),
            pltpu.VMEM((1, 1), jnp.int32),
            pltpu.VMEM((128, LANES), F32),
            pltpu.VMEM((128, LANES), F32),
            pltpu.VMEM((256, LANES), F32),
            pltpu.VMEM((256, LANES), F32),
            pltpu.VMEM((2, 12, 8, LANES), F32),
            pltpu.VMEM((2, 12, 8, LANES), F32),
            pltpu.VMEM((2, 8, 24, LANES), F32),
            pltpu.VMEM((8, 2, 24, LANES), F32),
            pltpu.VMEM((8, 2, 24, LANES), F32),
            pltpu.VMEM((12, 256, LANES), F32),
            pltpu.VMEM((8, 256, 256), F32),
            pltpu.VMEM((256, LANES), F32),
            pltpu.VMEM((256, LANES), F32),
            sems((8,)),
            sems((2,)),
            sems((2,)),
            sems((8,)),
            sems((8,)),
            sems((len(GATHER),)),
            sems((len(GATHER),)),
        ],
        compiler_params=pltpu.CompilerParams(collective_id=0, has_side_effects=True, vmem_limit_bytes=40 * 2**20),
        name="ladder",
    )(
        amplitudes,
        integrals,
        occ_energy.reshape(1, -1),
        vir_energy.reshape(1, -1),
        occ_irrep.reshape(1, -1),
        vir_irrep.reshape(1, -1),
        pair_irrep.reshape(1, -1),
        turn,
    )
    return out, most


def local(*args):
    turn = jnp.zeros((1, 1), jnp.int32)
    out, most = one_pass(turn, *args)

    def more(state):
        return (CAP * (state[0] + 1) < most)[0, 0]

    def step(state):
        turn = state[0] + 1
        return turn, state[1] + one_pass(turn, *args)[0]

    _, out = lax.while_loop(more, step, (turn, out))
    return jnp.transpose(out.reshape(8, 4, 64, 256), (1, 2, 0, 3))


def solution(mesh):
    placed = (P("occ", None, None), P("vir", "occ", None), P(), P(), P(), P(), P())
    return jax.shard_map(
        local, mesh=mesh, in_specs=placed, out_specs=P("occ", None, "vir", None), check_vma=False
    )
```

time: 44 us -> 40 us (0.909)
  Pallas kernels: 40.7 us -> 36.4 us
    pallas_call x1, Pallas kernels: 40.7 us -> 36.4 us  [one_pass(): pl.pallas_call(kernel, out_shape=(jax.ShapeDtypeStruct((8, 256, 256), F32...]
where the time goes in v3:
time: 40 us; the launch traced here: 39.6 us
  Pallas kernels  36.4 us (91%)
  local copies, waits for them, and re-layouts  2.54 us (6%)
  loops' own time  0.64 us (2%)
    pallas_call x1, Pallas kernels, one_pass(): pl.pallas_call(kernel, out_shape=(jax.ShapeDtypeStruct((8, 256, 256), F32...  36.4 us
    while x1, local copies, waits for them, and re-layouts, local(): _, out = lax.while_loop(more, step, (turn, out))  2.54 us

profile of v3, /device:TPU:1, one launch (start us, length us, event | category | flops | bytes accessed | tf_op | source)
XLA Modules:
  0.0 39.6 jit_solution(11331144367433072743)
XLA Ops:
  0.0 36.4 %ladder.2 = (f32[8,256,256]{2,1,0:T(8,128)S(1)}, s32[1,1]{1,0:T(1,128)}) custom-call(f32[4,64,1024]{2,1,0:T(8,128)} %t_hbm.1, f32[8,16,1024]{2,1,0:T(8,128)} %v_hbm.1, f32[1,64]{1,0:T(1,128)} %bitcast.26, f32[1,256]{1,0:T(1,128)} %bitcast.22, s32[1,64]{1,0:T(1,128)} %bitcast.28, s32[1,256]{1,0:T(1,128)} %bitcast.24, s32[1,1024]{1,0:T(1,128)} %bitcast.20, ...), custom_call_target="tpu_custom_call" | custom-call | tf_op jit(solution)/shard_map/ladder/pallas_call | solution.py:318
  36.4 0.6 %while.10 = (s32[1,1]{1,0:T(1,128)}, f32[8,256,256]{2,1,0:T(8,128)S(1)}, s32[1,1]{1,0:T(1,128)}, f32[64]{0:T(128)}, f32[256]{0:T(256)}, /*index=5*/s32[64]{0:T(1...) while((s32[1,1]{1,0:T(1,128)}, ...), condition=%wide.region_1.0_spmd, body=%wide.region_0.0_spmd | while | flops 524292 | bytes 6291589 | solution.py:382
  37.1 2.5 %copy.8 = f32[8,256,256]{2,0,1:T(8,128)} copy(f32[8,256,256]{2,1,0:T(8,128)S(1)} %get-tuple-element.63) | data formatting | bytes 4194304 | tf_op jit(solution)/shard_map/while | solution.py:382

commit v4 on v3

--- a/solution.py
+++ b/solution.py
@@ -20,10 +20,9 @@
 CORE = (0, 0, 1)
 CHIPS = (Z2, X2, ZP, ZM, XP, XM, Z)
 ROUTES = (
-    (OWN, X2), (OWN, Z), (OWN, XP), (OWN, XM), (OWN, CORE),
-    (Z, XP), (Z, XM), (Z, CORE),
+    (OWN, ZP), (OWN, ZM), (OWN, X2), (OWN, Z), (OWN, XP), (OWN, XM), (OWN, CORE),
     (X2, Z), (X2, CORE),
-    (XP, CORE), (XM, CORE), (ZM, CORE), (ZP, CORE), (Z2, CORE),
+    (Z, CORE), (XP, CORE), (XM, CORE), (ZM, CORE), (ZP, CORE), (Z2, CORE),
 )
 
 
@@ -38,6 +37,7 @@
 
 
 GATHER = gather_ops()
+LATE = 1
 
 
 def split(x):
@@ -228,7 +228,7 @@
     a_recv[chip] = a_pair[chip]
     lax.fori_loop(4, 8, weigh, 0)
 
-    here = pl.multiple_of(16 * occ, 16)
+    mine = blocks.at[occ]
     for g in range(2):
         from_self = jnp.logical_and(mirror_self, vir % 2 == g)
 
@@ -239,15 +239,15 @@
         for q in range(4):
             for t in range(2):
                 own = vm[pl.ds(16 * (q + 4 * t) + 8 * g, 8), :]
-                blocks[3 * q + t, pl.ds(here + 8 * g, 8), :] = own - t_recv[g, 3 * q + t]
+                mine[3 * q + t, pl.ds(8 * g, 8), :] = own - t_recv[g, 3 * q + t]
             own = jnp.where(first_half, vt[pl.ds(16 * q + 8 * g, 8), :], vt[pl.ds(16 * (q + 4) + 8 * g, 8), :])
-            blocks[3 * q + 2, pl.ds(here + 8 * g, 8), :] = own - t_recv[g, 3 * q + 2]
+            mine[3 * q + 2, pl.ds(8 * g, 8), :] = own - t_recv[g, 3 * q + 2]
 
     def hop(n, landing=False):
         whose, route, _ = GATHER[n]
         if landing:
             whose = tuple((k - r) % m for k, r, m in zip(whose, route, (4, 2, 2)))
-        part = blocks.at[:, pl.ds(pl.multiple_of(16 * member(whose), 16), 16), :]
+        part = blocks.at[member(whose)]
         return pltpu.make_async_remote_copy(
             src_ref=part,
             dst_ref=part,
@@ -267,6 +267,11 @@
     for n, (_, _, after) in enumerate(GATHER):
         if after is None:
             hop(n).start()
+
+    forwards = [n for n, (_, _, after) in enumerate(GATHER) if after is not None]
+    for n in forwards[:LATE]:
+        need(GATHER[n][2])
+        hop(n).start()
 
     for copy in swaps:
         copy.wait_recv()
@@ -285,19 +290,22 @@
         high, low = split(jnp.concatenate([a_main[...], kept], axis=1))
         factors.append(jnp.concatenate([high, low, high], axis=1))
 
-    for n, (_, _, after) in enumerate(GATHER):
-        if after is not None:
-            need(after)
-            hop(n).start()
+    for n in forwards[LATE:]:
+        need(GATHER[n][2])
+        hop(n).start()
     for n in range(len(GATHER)):
         need(n)
 
+    def rows_of(n):
+        return jnp.concatenate([blocks[o, n] for o in range(16)], axis=0)
+
     for q in range(4):
         for t in range(2):
-            high, low = split(jnp.concatenate([blocks[3 * q + t], blocks[3 * q + 2]], axis=1))
+            high, low = split(jnp.concatenate([rows_of(3 * q + t), rows_of(3 * q + 2)], axis=1))
             c = dot_t(factors[t], jnp.concatenate([high, high, low], axis=1))
-            out_ref[q + 4 * t] = c * weight[q + 4 * t]
-
+            c = c * weight[q + 4 * t]
+            for s in range(2):
+                out_ref[s, pl.ds(q + 4 * t, 256, stride=8), :] = c[:, 128 * s : 128 * (s + 1)]
     for h in range(2):
 
         @pl.when(jnp.logical_not(jnp.logical_and(mirror_self, vir % 2 == h)))
@@ -318,7 +326,7 @@
     out, most = pl.pallas_call(
         kernel,
         out_shape=(
-            jax.ShapeDtypeStruct((8, 256, 256), F32),
+            jax.ShapeDtypeStruct((2, 2048, LANES), F32),
             jax.ShapeDtypeStruct((1, 1), jnp.int32),
         ),
         in_specs=[away] * 8,
@@ -341,7 +349,7 @@
             pltpu.VMEM((2, 8, 24, LANES), F32),
             pltpu.VMEM((8, 2, 24, LANES), F32),
             pltpu.VMEM((8, 2, 24, LANES), F32),
-            pltpu.VMEM((12, 256, LANES), F32),
+            pltpu.VMEM((16, 12, 16, LANES), F32),
             pltpu.VMEM((8, 256, 256), F32),
             pltpu.VMEM((256, LANES), F32),
             pltpu.VMEM((256, LANES), F32),
@@ -368,6 +376,31 @@
     return out, most
 
 
+def place(src_ref, out_ref, sem):
+    copies = [
+        pltpu.make_async_copy(
+            src_ref.at[s, i], out_ref.at[i, :, :, pl.ds(128 * s, 128)], sem.at[4 * s + i]
+        )
+        for s in range(2)
+        for i in range(4)
+    ]
+    for copy in copies:
+        copy.start()
+    for copy in copies:
+        copy.wait()
+
+
+def lay_out(out):
+    return pl.pallas_call(
+        place,
+        out_shape=jax.ShapeDtypeStruct((4, 64, 8, 256), F32),
+        in_specs=[pl.BlockSpec(memory_space=pl.ANY)],
+        out_specs=pl.BlockSpec(memory_space=pltpu.HBM),
+        scratch_shapes=[pltpu.SemaphoreType.DMA((8,))],
+        name="lay_out",
+    )(out.reshape(2, 4, 64, 8, 128))
+
+
 def local(*args):
     turn = jnp.zeros((1, 1), jnp.int32)
     out, most = one_pass(turn, *args)
@@ -380,7 +413,7 @@
         return turn, state[1] + one_pass(turn, *args)[0]
 
     _, out = lax.while_loop(more, step, (turn, out))
-    return jnp.transpose(out.reshape(8, 4, 64, 256), (1, 2, 0, 3))
+    return lay_out(out)
 
 
 def solution(mesh):

time: 40 us -> 38.9 us (0.972)
  local copies, waits for them, and re-layouts: 2.54 us -> 0 us
  Pallas kernels: 36.4 us -> 38.1 us
    while x1 -> x0, local copies, waits for them, and re-layouts: 2.54 us -> none  [local(): _, out = lax.while_loop(more, step, (turn, out))]
    pallas_call x1 -> x2, Pallas kernels: 36.4 us -> 38.1 us  [the longest x1 36.7 us: one_pass(): pl.pallas_call(kernel, out_shape=(jax.ShapeDtypeStruct((2, 2048, LANES),...]
where the time goes in v4:
time: 38.9 us; the launch traced here: 38.8 us
  Pallas kernels  38.1 us (98%)
  loops' own time  0.64 us (2%)
    pallas_call x1, Pallas kernels, one_pass(): pl.pallas_call(kernel, out_shape=(jax.ShapeDtypeStruct((2, 2048, LANES),...  36.7 us
    pallas_call x1, Pallas kernels, lay_out(): pl.pallas_call(place, out_shape=jax.ShapeDtypeStruct((4, 64, 8, 256), F32...  1.38 us

profile of v4, /device:TPU:1, one launch (start us, length us, event | category | flops | bytes accessed | tf_op | source)
XLA Modules:
  0.0 38.8 jit_solution(6443655502400393326)
XLA Ops:
  0.0 36.7 %ladder.2 = (f32[2,2048,128]{2,1,0:T(8,128)S(1)}, s32[1,1]{1,0:T(1,128)}) custom-call(f32[4,64,1024]{2,1,0:T(8,128)} %t_hbm.1, f32[8,16,1024]{2,1,0:T(8,128)} %v_hbm.1, f32[1,64]{1,0:T(1,128)} %bitcast.25, f32[1,256]{1,0:T(1,128)} %bitcast.21, s32[1,64]{1,0:T(1,128)} %bitcast.27, s32[1,256]{1,0:T(1,128)} %bitcast.23, s32[1,1024]{1,0:T(1,128)} %bitcast.19, ...), custom_call_target="tpu_custom_call" | custom-call | tf_op jit(solution)/shard_map/ladder/pallas_call | solution.py:326
  36.7 0.6 %while.10 = (s32[1,1]{1,0:T(1,128)}, f32[2,2048,128]{2,1,0:T(8,128)S(1)}, s32[1,1]{1,0:T(1,128)}, f32[64]{0:T(128)}, f32[256]{0:T(256)}, /*index=5*/s32[64]{0:T(...) while((s32[1,1]{1,0:T(1,128)}, ...), condition=%wide.region_1.0_spmd, body=%wide.region_0.0_spmd | while | flops 524292 | bytes 6291589 | solution.py:415
  37.4 1.4 %lay_out.1 = f32[4,64,8,256]{3,2,1,0:T(8,128)} custom-call(f32[2,4,64,8,128]{4,3,2,1,0:T(8,128)S(1)} %bitcast.18), custom_call_target="tpu_custom_call" | custom-call | tf_op jit(solution)/shard_map/lay_out/pallas_call | solution.py:394

commit v5 on v4

--- a/solution.py
+++ b/solution.py
@@ -12,8 +12,10 @@
 BF16 = jnp.bfloat16
 
 LANES = 128
-TAIL = 64
+TAIL = 32
 CAP = LANES + TAIL
+PER = LANES // TAIL
+ROWS = 8 + 8 // PER
 
 OWN, XP, XM, X2 = (0, 0, 0), (1, 0, 0), (3, 0, 0), (2, 0, 0)
 Z, ZP, ZM, Z2 = (0, 1, 0), (1, 1, 0), (3, 1, 0), (2, 1, 0)
@@ -60,8 +62,8 @@
 
 def kernel(
     t_hbm, v_hbm, eo_hbm, ev_hbm, so_hbm, sv_hbm, pair_hbm, turn_hbm, out_ref, most_ref,
-    t_buf, v_buf, eo_ref, ev_ref, so_ref, sv_ref, pair_ref, turn_ref, vm, vt, tm, tt, t_send, t_recv, a_send, a_pair, a_recv,
-    blocks, weight, a_main, a_tail, in_sem, ts_sem, tr_sem, as_sem, ar_sem, gs_sem, gr_sem,
+    t_buf, v_buf, eo_ref, ev_ref, so_ref, sv_ref, pair_ref, turn_ref, vm, vt, tm, tt, raw, raw_formed, t_send, t_recv, a_send, a_pair, a_recv,
+    blocks, weight, a_main, a_tail, in_sem, raw_sem, ts_sem, tr_sem, as_sem, ar_sem, gs_sem, gr_sem,
 ):
     occ, vir = lax.axis_index("occ"), lax.axis_index("vir")
     x, zl, core = occ // 4, (occ // 2) % 2, occ % 2
@@ -69,15 +71,18 @@
     def member(step):
         return ((x + step[0]) % 4) * 4 + ((zl + step[1]) % 2) * 2 + (core + step[2]) % 2
 
-    mirror_occ = vir // 2
-    mirror_self = mirror_occ == occ
+    z_hi = vir // 8
+
+    def block_of(step):
+        return ((6 + 2 * z_hi - x - step[0]) % 4) * 4 + ((zl + step[1]) % 2) * 2 + (core + step[2]) % 2
+
+    formed = block_of(OWN)
+    moved = formed != occ
+    mirror_occ = ((6 + 2 * x - z_hi) % 4) * 4 + (vir % 8) // 2
+
     bar = pltpu.get_barrier_semaphore()
-    for h in range(2):
-
-        @pl.when(jnp.logical_not(jnp.logical_and(mirror_self, vir % 2 == h)))
-        def _():
-            pl.semaphore_signal(bar, inc=1, device_id={"occ": mirror_occ, "vir": 2 * occ + h}, device_id_type=MESH)
-
+    for g in range(2):
+        pl.semaphore_signal(bar, inc=1, device_id={"occ": vir // 2, "vir": 2 * formed + g}, device_id_type=MESH)
     for step in CHIPS + (CORE,):
         pl.semaphore_signal(bar, inc=1, device_id={"occ": member(step)}, device_id_type=MESH)
 
@@ -99,25 +104,33 @@
     hot = jnp.where(pair == lax.broadcasted_iota(jnp.int32, (8, pair.shape[1]), 0), 1.0, 0.0)
     upper = lax.broadcasted_iota(jnp.int32, (128, 128), 0) <= lax.broadcasted_iota(jnp.int32, (128, 128), 1)
     upper = jnp.where(upper, 1.0, 0.0).astype(BF16)
-    parts = [hot[:, 128 * c : 128 * (c + 1)] for c in range(8)]
-    counted = jnp.dot(jnp.concatenate(parts, axis=0).astype(BF16), upper, preferred_element_type=F32)
-    before = jnp.zeros((8, 1), F32)
-    ranks = []
-    for c in range(8):
-        here = counted[8 * c : 8 * (c + 1)]
-        ranks.append(jnp.sum(parts[c] * (here + before), axis=0, keepdims=True))
-        before = before + here[:, 127:128]
-    rank = jnp.concatenate(ranks, axis=1) - 1.0 - CAP * turn_ref[...].astype(F32)
-    most_ref[...] = jnp.broadcast_to(jnp.max(before, axis=0, keepdims=True), most_ref.shape).astype(jnp.int32)
+    parts = jnp.concatenate([hot[:, 128 * c : 128 * (c + 1)] for c in range(8)], axis=0)
+    counted = jnp.dot(parts.astype(BF16), jnp.concatenate([upper, jnp.ones_like(upper)], axis=1), preferred_element_type=F32)
+    run, of = lax.broadcasted_iota(jnp.int32, (64, 64), 0), lax.broadcasted_iota(jnp.int32, (64, 64), 1)
+    earlier = jnp.where(jnp.logical_and(run % 8 == of % 8, of < run), 1.0, 0.0).astype(BF16)
+    before = jnp.dot(earlier, counted[:, 128:].astype(BF16), preferred_element_type=F32)
+    spots = parts * (counted[:, :128] + before)
+    rank = jnp.concatenate([jnp.sum(spots[8 * c : 8 * (c + 1)], axis=0, keepdims=True) for c in range(8)], axis=1)
+    rank = rank - 1.0 - CAP * turn_ref[...].astype(F32)
+    total = (counted[56:, 128:] + before[56:])[:, :1]
+    most_ref[...] = jnp.max(total, axis=0, keepdims=True).astype(jnp.int32)
     lane_of = iota_col(2 * LANES)
-    lane_of = jnp.where(lane_of < CAP, lane_of, lane_of - TAIL).astype(F32)
+    lane_of = jnp.where(lane_of < LANES, lane_of, LANES + lane_of % TAIL).astype(F32)
     place = jnp.where(rank == lane_of, 1.0, 0.0).astype(BF16)
 
-    first_half = lax.broadcasted_iota(jnp.int32, (1, LANES), 1) < TAIL
+    lanes = lax.broadcasted_iota(jnp.int32, (1, LANES), 1)
+    first_half = lanes < LANES // 2
+
+    def side_by_side(tails):
+        out = tails[0]
+        for n in range(1, PER):
+            out = jnp.where(lanes < n * TAIL, out, tails[n])
+        return out
 
     def compact(values, sym):
         high, low = split(jnp.where(pair == sym, values, 0.0))
-        return dot_t(high, place) + dot_t(low, place)
+        both = dot_t(jnp.concatenate([high, low], axis=0), place)
+        return both[: len(sym)] + both[len(sym) :]
 
     loads[2].wait()
     sv_row = sv_ref[...].astype(F32)
@@ -128,20 +141,12 @@
     vm[...] = small[:, :LANES]
     vt[...] = small[:, LANES:]
     for h in range(2):
-        for q in range(4):
-            for t in range(2):
-                t_send[h, 3 * q + t] = vm[pl.ds(8 * h + q + 4 * t, 8, stride=16), :]
-            t_send[h, 3 * q + 2] = jnp.where(
-                first_half, vt[pl.ds(8 * h + q, 8, stride=16), :], vt[pl.ds(8 * h + q + 4, 8, stride=16), :]
-            )
-
-    @pl.when(mirror_self)
-    def _():
-        pl.semaphore_wait(bar, 9)
-
-    @pl.when(jnp.logical_not(mirror_self))
-    def _():
-        pl.semaphore_wait(bar, 10)
+        for a in range(8):
+            t_send[h, a] = vm[pl.ds(8 * h + a, 8, stride=16), :]
+        for u in range(8 // PER):
+            t_send[h, 8 + u] = side_by_side([vt[pl.ds(8 * h + PER * u + n, 8, stride=16), :] for n in range(PER)])
+
+    pl.semaphore_wait(bar, len(CHIPS) + 3)
 
     def mirror(h, slot):
         return pltpu.make_async_remote_copy(
@@ -154,15 +159,28 @@
         )
 
     for h in range(2):
-        to_self = jnp.logical_and(mirror_self, vir % 2 == h)
-
-        @pl.when(to_self)
-        def _():
-            t_recv[h] = t_send[h]
-
-        @pl.when(jnp.logical_not(to_self))
-        def _():
-            mirror(h, vir % 2).start()
+        mirror(h, vir % 2).start()
+
+    for a in range(8):
+        raw[a] = vm[pl.ds(16 * a, 16), :]
+    for u in range(8 // PER):
+        raw[8 + u] = side_by_side([vt[pl.ds(16 * (PER * u + n), 16), :] for n in range(PER)])
+    cross = pltpu.make_async_remote_copy(
+        src_ref=raw,
+        dst_ref=raw_formed,
+        send_sem=raw_sem.at[0],
+        recv_sem=raw_sem.at[1],
+        device_id={"occ": formed},
+        device_id_type=MESH,
+    )
+
+    @pl.when(moved)
+    def _():
+        cross.start()
+
+    @pl.when(jnp.logical_not(moved))
+    def _():
+        raw_formed[...] = raw[...]
 
     loads[4].wait()
     so_row = so_ref[...].astype(F32)
@@ -217,7 +235,9 @@
         which = jnp.full((1, 1), 8 * vir + a, jnp.int32)
         sym_b = sv_int ^ at_lane(sv_row, which).astype(jnp.int32)
         e_b = at_lane(ev_row, which) + ev_row
-        weight[a] = jnp.where(sym_t == sym_b, 1.0 / (e_ij - e_b), 0.0)
+        denom = e_ij - e_b
+        guess = pl.reciprocal(denom, approx=True)
+        weight[a] = jnp.where(sym_t == sym_b, guess * (2.0 - denom * guess), 0.0)
         return carry
 
     lax.fori_loop(0, 4, weigh, 0)
@@ -228,26 +248,20 @@
     a_recv[chip] = a_pair[chip]
     lax.fori_loop(4, 8, weigh, 0)
 
-    mine = blocks.at[occ]
+    @pl.when(moved)
+    def _():
+        cross.wait_recv()
+
     for g in range(2):
-        from_self = jnp.logical_and(mirror_self, vir % 2 == g)
-
-        @pl.when(jnp.logical_not(from_self))
-        def _():
-            mirror(g, g).wait_recv()
-
-        for q in range(4):
-            for t in range(2):
-                own = vm[pl.ds(16 * (q + 4 * t) + 8 * g, 8), :]
-                mine[3 * q + t, pl.ds(8 * g, 8), :] = own - t_recv[g, 3 * q + t]
-            own = jnp.where(first_half, vt[pl.ds(16 * q + 8 * g, 8), :], vt[pl.ds(16 * (q + 4) + 8 * g, 8), :])
-            mine[3 * q + 2, pl.ds(8 * g, 8), :] = own - t_recv[g, 3 * q + 2]
+        mirror(g, g).wait_recv()
+        rows = pl.ds(8 * g, 8)
+        blocks[formed, :, rows, :] = raw_formed[:, rows, :] - t_recv[g]
 
     def hop(n, landing=False):
         whose, route, _ = GATHER[n]
         if landing:
             whose = tuple((k - r) % m for k, r, m in zip(whose, route, (4, 2, 2)))
-        part = blocks.at[member(whose)]
+        part = blocks.at[block_of(whose)]
         return pltpu.make_async_remote_copy(
             src_ref=part,
             dst_ref=part,
@@ -281,12 +295,12 @@
             to = pl.ds(64 * i + j, 16, stride=4)
             a_main[to, :] = tm[to, :] - theirs[pl.ds(4 * j + i, 16, stride=24), :]
             tail = theirs[pl.ds(16 + 2 * j + i % 2, 16, stride=24), :]
-            turned = pltpu.roll(tail, TAIL, 1)
+            turned = pltpu.roll(tail, LANES // 2, 1)
             tail = jnp.where(first_half, tail, turned) if i < 2 else jnp.where(first_half, turned, tail)
             a_tail[to, :] = tt[to, :] - tail
     factors = []
-    for t in range(2):
-        kept = jnp.where(first_half if t == 0 else jnp.logical_not(first_half), a_tail[...], 0.0)
+    for n in range(PER):
+        kept = jnp.where(lanes // TAIL == n, a_tail[...], 0.0)
         high, low = split(jnp.concatenate([a_main[...], kept], axis=1))
         factors.append(jnp.concatenate([high, low, high], axis=1))
 
@@ -299,18 +313,17 @@
     def rows_of(n):
         return jnp.concatenate([blocks[o, n] for o in range(16)], axis=0)
 
-    for q in range(4):
-        for t in range(2):
-            high, low = split(jnp.concatenate([rows_of(3 * q + t), rows_of(3 * q + 2)], axis=1))
-            c = dot_t(factors[t], jnp.concatenate([high, high, low], axis=1))
-            c = c * weight[q + 4 * t]
-            for s in range(2):
-                out_ref[s, pl.ds(q + 4 * t, 256, stride=8), :] = c[:, 128 * s : 128 * (s + 1)]
+    for a in range(8):
+        high, low = split(jnp.concatenate([rows_of(a), rows_of(8 + a // PER)], axis=1))
+        c = dot_t(factors[a % PER], jnp.concatenate([high, high, low], axis=1)) * weight[a]
+        for s in range(2):
+            out_ref[s, pl.ds(a, 256, stride=8), :] = c[:, 128 * s : 128 * (s + 1)]
     for h in range(2):
-
-        @pl.when(jnp.logical_not(jnp.logical_and(mirror_self, vir % 2 == h)))
-        def _():
-            mirror(h, vir % 2).wait_send()
+        mirror(h, vir % 2).wait_send()
+
+    @pl.when(moved)
+    def _():
+        cross.wait_send()
 
     share.wait_send()
     for copy in swaps:
@@ -344,16 +357,19 @@
             pltpu.VMEM((128, LANES), F32),
             pltpu.VMEM((256, LANES), F32),
             pltpu.VMEM((256, LANES), F32),
-            pltpu.VMEM((2, 12, 8, LANES), F32),
-            pltpu.VMEM((2, 12, 8, LANES), F32),
+            pltpu.VMEM((ROWS, 16, LANES), F32),
+            pltpu.VMEM((ROWS, 16, LANES), F32),
+            pltpu.VMEM((2, ROWS, 8, LANES), F32),
+            pltpu.VMEM((2, ROWS, 8, LANES), F32),
             pltpu.VMEM((2, 8, 24, LANES), F32),
             pltpu.VMEM((8, 2, 24, LANES), F32),
             pltpu.VMEM((8, 2, 24, LANES), F32),
-            pltpu.VMEM((16, 12, 16, LANES), F32),
+            pltpu.VMEM((16, ROWS, 16, LANES), F32),
             pltpu.VMEM((8, 256, 256), F32),
             pltpu.VMEM((256, LANES), F32),
             pltpu.VMEM((256, LANES), F32),
             sems((8,)),
+            sems((2,)),
             sems((2,)),
             sems((2,)),
             sems((8,)),

time: 38.9 us -> 36.9 us (0.949); the launches traced: 38.8 us -> 36.3 us
  Pallas kernels: 38.1 us -> 35.7 us
    pallas_call x1, Pallas kernels: 36.7 us -> 34.3 us  [one_pass(): pl.pallas_call(kernel, out_shape=(jax.ShapeDtypeStruct((2, 2048, LANES),...]
where the time goes in v5:
time: 36.9 us; the launch traced here: 36.3 us
  Pallas kernels  35.7 us (97%)
  loops' own time  0.64 us (2%)
    pallas_call x1, Pallas kernels, one_pass(): pl.pallas_call(kernel, out_shape=(jax.ShapeDtypeStruct((2, 2048, LANES),...  34.3 us
    pallas_call x1, Pallas kernels, lay_out(): pl.pallas_call(place, out_shape=jax.ShapeDtypeStruct((4, 64, 8, 256), F32...  1.38 us

profile of v5, /device:TPU:1, one launch (start us, length us, event | category | flops | bytes accessed | tf_op | source)
XLA Modules:
  0.0 36.3 jit_solution(15041680003735903504)
XLA Ops:
  0.0 34.3 %ladder.2 = (f32[2,2048,128]{2,1,0:T(8,128)S(1)}, s32[1,1]{1,0:T(1,128)}) custom-call(f32[4,64,1024]{2,1,0:T(8,128)} %t_hbm.1, f32[8,16,1024]{2,1,0:T(8,128)} %v_hbm.1, f32[1,64]{1,0:T(1,128)} %bitcast.25, f32[1,256]{1,0:T(1,128)} %bitcast.21, s32[1,64]{1,0:T(1,128)} %bitcast.27, s32[1,256]{1,0:T(1,128)} %bitcast.23, s32[1,1024]{1,0:T(1,128)} %bitcast.19, ...), custom_call_target="tpu_custom_call" | custom-call | tf_op jit(solution)/shard_map/ladder/pallas_call | solution.py:339
  34.3 0.6 %while.10 = (s32[1,1]{1,0:T(1,128)}, f32[2,2048,128]{2,1,0:T(8,128)S(1)}, s32[1,1]{1,0:T(1,128)}, f32[64]{0:T(128)}, f32[256]{0:T(256)}, /*index=5*/s32[64]{0:T(...) while((s32[1,1]{1,0:T(1,128)}, ...), condition=%wide.region_1.0_spmd, body=%wide.region_0.0_spmd | while | flops 524292 | bytes 6291589 | solution.py:431
  35.0 1.4 %lay_out.1 = f32[4,64,8,256]{3,2,1,0:T(8,128)} custom-call(f32[2,4,64,8,128]{4,3,2,1,0:T(8,128)S(1)} %bitcast.18), custom_call_target="tpu_custom_call" | custom-call | tf_op jit(solution)/shard_map/lay_out/pallas_call | solution.py:410

commit v6 on v5

--- a/solution.py
+++ b/solution.py
@@ -22,9 +22,9 @@
 CORE = (0, 0, 1)
 CHIPS = (Z2, X2, ZP, ZM, XP, XM, Z)
 ROUTES = (
-    (OWN, ZP), (OWN, ZM), (OWN, X2), (OWN, Z), (OWN, XP), (OWN, XM), (OWN, CORE),
-    (X2, Z), (X2, CORE),
-    (Z, CORE), (XP, CORE), (XM, CORE), (ZM, CORE), (ZP, CORE), (Z2, CORE),
+    (OWN, X2), (OWN, ZP), (OWN, ZM), (OWN, Z), (OWN, XP), (OWN, XM), (OWN, CORE),
+    (X2, Z),
+    (Z, CORE), (XP, CORE), (XM, CORE), (X2, CORE), (ZM, CORE), (ZP, CORE), (Z2, CORE),
 )
 
 

time: 36.9 us -> 36.9 us (level)
  no operation moved by 1% of the time
where the time goes in v6:
time: 36.9 us; the launch traced here: 36.3 us
  Pallas kernels  35.7 us (97%)
  loops' own time  0.64 us (2%)
    pallas_call x1, Pallas kernels, one_pass(): pl.pallas_call(kernel, out_shape=(jax.ShapeDtypeStruct((2, 2048, LANES),...  34.3 us
    pallas_call x1, Pallas kernels, lay_out(): pl.pallas_call(place, out_shape=jax.ShapeDtypeStruct((4, 64, 8, 256), F32...  1.38 us

profile of v6, /device:TPU:1, one launch (start us, length us, event | category | flops | bytes accessed | tf_op | source)
XLA Modules:
  0.0 36.3 jit_solution(13175144304427017783)
XLA Ops:
  0.0 34.3 %ladder.2 = (f32[2,2048,128]{2,1,0:T(8,128)S(1)}, s32[1,1]{1,0:T(1,128)}) custom-call(f32[4,64,1024]{2,1,0:T(8,128)} %t_hbm.1, f32[8,16,1024]{2,1,0:T(8,128)} %v_hbm.1, f32[1,64]{1,0:T(1,128)} %bitcast.25, f32[1,256]{1,0:T(1,128)} %bitcast.21, s32[1,64]{1,0:T(1,128)} %bitcast.27, s32[1,256]{1,0:T(1,128)} %bitcast.23, s32[1,1024]{1,0:T(1,128)} %bitcast.19, ...), custom_call_target="tpu_custom_call" | custom-call | tf_op jit(solution)/shard_map/ladder/pallas_call | solution.py:339
  34.3 0.6 %while.10 = (s32[1,1]{1,0:T(1,128)}, f32[2,2048,128]{2,1,0:T(8,128)S(1)}, s32[1,1]{1,0:T(1,128)}, f32[64]{0:T(128)}, f32[256]{0:T(256)}, /*index=5*/s32[64]{0:T(...) while((s32[1,1]{1,0:T(1,128)}, ...), condition=%wide.region_1.0_spmd, body=%wide.region_0.0_spmd | while | flops 524292 | bytes 6291589 | solution.py:431
  35.0 1.4 %lay_out.1 = f32[4,64,8,256]{3,2,1,0:T(8,128)} custom-call(f32[2,4,64,8,128]{4,3,2,1,0:T(8,128)S(1)} %bitcast.18), custom_call_target="tpu_custom_call" | custom-call | tf_op jit(solution)/shard_map/lay_out/pallas_call | solution.py:410
